TPU v7x, 512 devices: a whole 4x4x16 slice. The times are simulated.
512 devices in a mesh: seg: 16 (over z_lo, x), dp: 32 (over y, z_hi, core).
Axes of the slice: x: 4, y: 4, z: 16 (z_hi: 4, z_lo: 4; z = z_hi * 4 + z_lo), core: 2. Of those that a mesh axis runs over, the one named last changes fastest.
Arguments:
- tokens: bfloat16 [16, 32, 128, 4096], P('seg', 'dp'), may hold values from -6 to 6
- cotangent: bfloat16 [16, 32, 128, 4096], P('seg', 'dp'), may hold values from -6 to 6
- query_weight: bfloat16 [4096, 64], P('dp'), may hold values from -0.09375 to 0.09375
- key_weight: bfloat16 [4096, 64], P('dp'), may hold values from -0.09375 to 0.09375
- forget_rate: float32 [16, 32, 64], P('seg', 'dp'), may hold values from 0.003 to 0.6
- resets: int32 [16, 32], P('seg', 'dp'), may hold values 0 or 1
Outputs:
- output: bfloat16 [16, 32, 128, 4096], P('seg', 'dp')
- input_grad: bfloat16 [16, 32, 128, 4096], P('seg', 'dp')
- grad_query: float32 [4096, 64], P(('seg', 'dp'))
- grad_key: float32 [4096, 64], P(('seg', 'dp'))
Inputs may be any that keep to these rules, and one draw needn't show every extreme that they name: `resets`: 1 where the segment is the last of its document.
All inputs are finite; a program needn't handle non-finite values. No bound on the sum of `resets` on one device may be relied on, other than what follows from the above.
Results may differ from a plain program's by a relative error of at most 0.0057.
Values may be sent and summed in bfloat16 or wider, within the bound.
A program may use at most 128 MiB of HBM per device.

v0:
```python
import jax
import jax.numpy as jnp
from jax import lax
from jax.sharding import PartitionSpec as P


def prefix(array, axis, combine, identity, reverse):
    devices, position = (lax.axis_size(axis), lax.axis_index(axis))
    everything = jax.tree.map(lambda part: lax.all_gather(part, axis), array)
    start = jax.tree.map(
        lambda part, zero: jnp.broadcast_to(jnp.asarray(zero, part.dtype), part.shape),
        array,
        identity,
    )

    def step(k, before):
        at = devices - 1 - k if reverse else k
        reached = at > position if reverse else at < position
        new = combine(before, jax.tree.map(lambda part: part[at], everything))
        return jax.tree.map(lambda a, b: jnp.where(reached, a, b), new, before)

    return lax.fori_loop(0, devices, step, start)


def feature(values):
    return jnp.where(values > 0, values + 1.0, jnp.exp(jnp.minimum(values, 0.0)))


def feature_slope(values):
    return jnp.where(values > 0, 1.0, jnp.exp(jnp.minimum(values, 0.0)))


def forward_join(earlier, later):
    return (earlier[0] * later[0], later[0][:, None] * earlier[1] + later[1])


def backward_join(earlier, later):
    return (earlier[0] * later[0], later[1] + later[0][:, None] * earlier[1])


def local(tokens, cotangent, query_weight, key_weight, forget_rate, resets):
    input_rows = tokens[0, 0]
    output_gradient = cotangent[0, 0]
    key_width = query_weight.shape[1]
    row_total = input_rows.shape[0]
    stacked = jnp.concatenate([query_weight, key_weight], axis=1)
    columns = input_rows
    both = jnp.dot(
        columns,
        lax.all_gather(stacked, "dp", axis=0, tiled=True),
        preferred_element_type=jnp.float32,
    )
    queries = both[:, :key_width]
    keys = both[:, key_width:]
    query_features = feature(queries).astype(jnp.bfloat16)
    key_features = feature(keys).astype(jnp.bfloat16)
    retain = jnp.exp(-forget_rate[0, 0]) * (1 - resets[0, 0]).astype(jnp.float32)
    memory_update = (
        jnp.dot(key_features.T, input_rows, preferred_element_type=jnp.float32) / row_total
    )
    neutral = (jnp.ones((key_width,), jnp.float32), jnp.zeros(memory_update.shape, jnp.float32))
    memory_in = prefix((retain, memory_update), "seg", forward_join, neutral, False)[1]
    memory_readout = memory_in.astype(jnp.bfloat16)
    output = (
        input_rows.astype(jnp.float32)
        + jnp.dot(query_features, memory_readout, preferred_element_type=jnp.float32)
    ).astype(jnp.bfloat16)
    memory_gradient = jnp.dot(query_features.T, output_gradient, preferred_element_type=jnp.float32)
    readout_gradient = lax.dot_general(
        output_gradient,
        memory_readout,
        (((1,), (1,)), ((), ())),
        preferred_element_type=jnp.float32,
    )
    query_grad = (readout_gradient * feature_slope(queries)).astype(jnp.bfloat16)
    update_grad = prefix((retain, memory_gradient), "seg", backward_join, neutral, True)[1]
    update_readout = update_grad.astype(jnp.bfloat16)
    feature_gradient = (
        lax.dot_general(
            input_rows, update_readout, (((1,), (1,)), ((), ())), preferred_element_type=jnp.float32
        )
        / row_total
    )
    key_grad = (feature_gradient * feature_slope(keys)).astype(jnp.bfloat16)
    writing_gradient = (
        jnp.dot(key_features, update_readout, preferred_element_type=jnp.float32) / row_total
    )
    both_grad = jnp.concatenate([query_grad, key_grad], axis=1)
    projected = lax.dot_general(
        both_grad,
        lax.all_gather(stacked, "dp", axis=0, tiled=True),
        (((1,), (1,)), ((), ())),
        preferred_element_type=jnp.float32,
    )
    input_grad = (output_gradient.astype(jnp.float32) + writing_gradient + projected).astype(
        jnp.bfloat16
    )
    columns = input_rows
    summed = lax.psum_scatter(
        lax.dot_general(
            columns, both_grad, (((0,), (0,)), ((), ())), preferred_element_type=jnp.float32
        ),
        ("seg", "dp"),
        scatter_dimension=0,
        tiled=True,
    )
    grad_query = summed[:, :key_width]
    grad_key = summed[:, key_width:]
    return (output[None, None], input_grad[None, None], grad_query, grad_key)


def solution(mesh):
    placed = (
        P("seg", "dp", None, None),
        P("seg", "dp", None, None),
        P("dp", None),
        P("dp", None),
        P("seg", "dp", None),
        P("seg", "dp"),
    )
    return jax.shard_map(
        local,
        mesh=mesh,
        in_specs=placed,
        out_specs=(
            P("seg", "dp", None, None),
            P("seg", "dp", None, None),
            P(("seg", "dp"), None),
            P(("seg", "dp"), None),
        ),
        check_vma=False,
    )
```

profile of v0, /device:TPU:1, one launch (start us, length us, event | category | flops | bytes accessed | tf_op | source)
XLA Modules:
  0.0 983.6 jit_solution(13976787727428415086)
XLA Ops:
  7.2 1.4 pad_maximum_fusion
  8.7 81.2 %all-gather.7.cloned.1.call-done = bf16[4096,128]{0,1:T(8,128)(2,1)} async-done(((bf16[128,128]{0,1:T(8,128)(2,1)}), bf16[4096,128]{0,1:T(8,128)(2,1)}) %all-gather.7.cloned.1.call-update) | async-done | bytes 1048592 | tf_op jit(solution)/shard_map/all_gather | solution.py:50
  89.9 2.0 convolution_bitcast_fusion.1
  91.9 1.3 fusion.13
  93.3 1.3 convolution_multiply_fusion.1
  95.3 37.5 %all-gather = f32[16,1,64]{2,1,0:T(1,128)S(1)} all-gather(f32[1,1,64]{2,1,0:T(1,128)S(1)} %exponential_multiply_fusion), channel_id=2, replica_groups=mesh['seg'=16,'dp'=32] {'seg'}, dimensions={0}, use_global_device_ids=true | all-gather | bytes 4352 | tf_op jit(solution)/shard_map/all_gather | solution.py:9
  132.8 148.5 %all-gather.11.cloned.1.call-done = f32[1024,4096]{1,0:T(8,128)} async-done(((f32[64,4096]{1,0:T(8,128)}), f32[1024,4096]{1,0:T(8,128)}) %all-gather.11.cloned.1.call-update) | async-done | bytes 16777232 | tf_op jit(solution)/shard_map/all_gather | solution.py:9
  281.3 26.1 %while.31 = (s32[]{:T(128)}, f32[64,4096]{1,0:T(8,128)S(1)}, s32[]{:T(128)}, f32[16,64,4096]{2,1,0:T(8,128)}, f32[16,64]{1,0:T(8,128)S(1)}, /*index=5*/s32[]{:T(128)}, s32[]{:T(128)}, s32[]{:T(128)}, s32[]{:T(128)}) while((s32[]{:T(128)}, f32[64,4096]{1,0:T(8,128)S(1)}, s32[]{:T(128)}, f32[16,64,4096]{2,1,0:T(8,128)}, ...), condition=%wide.region_3.4_spmd.clone, body=%wide.region_2.3_spmd.clone.sunk | while | flops 1048584 | bytes 3146663 | solution.py:22
  281.3 1.6 fusion.31
  282.9 1.6 fusion.31
  284.6 1.6 fusion.31
  286.2 1.6 fusion.31
  287.8 1.6 fusion.31
  289.5 1.6 fusion.31
  291.1 1.6 fusion.31
  292.7 1.6 fusion.31
  294.3 1.6 fusion.31
  296.0 1.6 fusion.31
  297.6 1.7 fusion.31
  299.3 1.6 fusion.31
  301.0 1.6 fusion.31
  302.6 1.6 fusion.31
  304.2 1.6 fusion.31
  305.9 1.6 fusion.31
  307.9 164.7 %all-gather.9.cloned.1.call-done = f32[1024,4096]{1,0:T(8,128)} async-done(((f32[64,4096]{1,0:T(8,128)}), f32[1024,4096]{1,0:T(8,128)}) %all-gather.9.cloned.1.call-update) | async-done | bytes 16777232 | tf_op jit(solution)/shard_map/all_gather | solution.py:9
  472.6 25.9 %while.30 = (s32[]{:T(128)}, f32[64,4096]{1,0:T(8,128)S(1)}, s32[]{:T(128)}, f32[16,64]{1,0:T(8,128)S(1)}, f32[16,64,4096]{2,1,0:T(8,128)}, /*index=5*/s32[]{:T(128)}, s32[]{:T(128)}) while((s32[]{:T(128)}, f32[64,4096]{1,0:T(8,128)S(1)}, s32[]{:T(128)}, f32[16,64]{1,0:T(8,128)S(1)}, f32[16,64,4096]{2,1,0:T(8,128)}, ...), condition=%wide.region_1.2_spmd.clone, body=%wide.region_0.1_spmd.clone.sunk | while | flops 1048580 | bytes 3146601 | solution.py:22
  472.6 1.6 fusion.30
  474.2 1.6 fusion.30
  475.8 1.6 fusion.30
  477.5 1.6 fusion.30
  479.1 1.6 fusion.30
  480.7 1.6 fusion.30
  482.3 1.6 fusion.30
  483.9 1.6 fusion.30
  485.6 1.6 fusion.30
  487.2 1.6 fusion.30
  488.8 1.6 fusion.30
  490.4 1.6 fusion.30
  492.0 1.6 fusion.30
  493.6 1.6 fusion.30
  495.3 1.6 fusion.30
  496.9 1.6 fusion.30
  498.5 1.7 fusion.11
  500.2 1.7 convolution_bitcast_fusion
  502.0 1.4 fusion.6
  504.6 1.4 fusion.5
  506.1 468.8 %all-reduce.3.cloned.1.call-done = f32[4096,128]{0,1:T(8,128)} async-done(((f32[4096,128]{0,1:T(8,128)}), f32[4096,128]{0,1:T(8,128)}) %all-reduce.3.cloned.1.call-update) | async-done | bytes 2097168
  974.9 0.9 fusion.25
  (58 shorter events, 3.6 us)
Async XLA Ops:
  7.2 84.8 %copy-start.1 = (bf16[1,1,128,4096]{3,2,1,0:T(8,128)(2,1)S(1)}, bf16[1,1,128,4096]{3,2,1,0:T(8,128)(2,1)}, u32[]{:S(2)}) copy-start(bf16[1,1,128,4096]{3,2,1,0:T(8,128)(2,1)} %param.11) | copy-start | bytes 3145732
  7.2 82.7 %all-gather.7.cloned.1.call-start = ((), (), s32[]{:S(2)}) async-start(), calls=%async_computation | async-start | bytes 1081344 | tf_op jit(solution)/shard_map/all_gather | solution.py:50
  8.7 272.6 %all-gather.11.cloned.1.call-start = ((), (), s32[]{:S(2)}) async-start(), calls=%async_computation.2 | async-start | bytes 17825792 | tf_op jit(solution)/shard_map/all_gather | solution.py:9
  91.9 1.4 copy-start
  93.2 2.1 copy-start.4
  93.2 379.4 %all-gather.9.cloned.1.call-start = ((), (), s32[]{:S(2)}) async-start(), calls=%async_computation.1 | async-start | bytes 17825792 | tf_op jit(solution)/shard_map/all_gather | solution.py:9
  94.6 880.3 %all-reduce.3.cloned.1.call-start = ((), (), s32[]{:S(2)}) async-start(), calls=%async_computation.3 | async-start | bytes 4194304
  502.0 1.5 copy-start.2
  503.4 1.2 copy-start.3
Sparse Core Ops, SparseCore 0:
  11.6 78.2 all-gather.6
  93.3 187.8 all-gather.10
  284.0 188.6 all-gather.8
  502.1 472.7 all-reduce.2
where the time goes:
time: 985 us; the launch traced here: 984 us
  waiting for transfers between devices  863 us (88%)
  other arithmetic  52 us (5%)
  blocking collectives  37.5 us (4%)
  between operations  14.6 us (1%)
  matrix products  11.8 us (1%)
    unnamed x5, waiting for transfers between devices  469 us
    all_gather x2, waiting for transfers between devices, prefix(): everything = jax.tree.map(lambda part: lax.all_gather(part, axis), array)  313 us
    all_gather x1, waiting for transfers between devices, local(): lax.all_gather(stacked, 'dp', axis=0, tiled=True)  81.2 us
    select_n x32, other arithmetic, step(): return jax.tree.map(lambda a, b: jnp.where(reached, a, b), new, before)  50.6 us
    all_gather x1, blocking collectives, prefix(): everything = jax.tree.map(lambda part: lax.all_gather(part, axis), array)  37.5 us
  transfers between devices with their start and end apart: 4, of which 4 were waited for; matrix products, arithmetic and copies ran while one was open for 3% of the time, Pallas kernels for 0%

commit v1 on v0

v1 whole, which is shorter than its diff:
```python
import jax
import jax.numpy as jnp
from jax import lax
from jax.experimental import pallas as pl
from jax.experimental.pallas import tpu as pltpu
from jax.sharding import PartitionSpec as P

ZL, X = 4, 4
Y, ZH, C = 4, 4, 2
CHUNKS = 4
KEY = 64
F32 = jnp.float32
BF16 = jnp.bfloat16
MESH = pl.DeviceIdType.MESH


def dot(a, b, ca, cb):
    return lax.dot_general(a, b, (((ca,), (cb,)), ((), ())), preferred_element_type=F32)


def body(
    tok, cot, wq, wk, rate, reset,
    out, igrad, gq, gk,
    w, rt, sin, rin, zs, zr, sb, read, feat, slope, bg,
    gown, gsnd, grcv, hb, r1a, r1b, acc1a, acc1b, h1a, h1b, r2a, r2b, fin, r3,
    a1, a2, a3, a4, rx, rz, s_in, s_z, s_bk, s_c, e1a, e1b, e2a, e2b, e3,
):
    rows, width = tok.shape
    shard = wq.shape[0]
    xs = shard // X
    half = ZL // 2
    wide = width // (CHUNKS * X)
    s = lax.axis_index("seg")
    b = lax.axis_index("dp")
    zl, x = s // X, s % X
    y, zh, c = b // (ZH * C), (b // C) % ZH, b % C

    def dev(zl=zl, x=x, y=y, zh=zh, c=c):
        return (zl * X + x, (y * ZH + zh) * C + c)

    started = []

    def send(src, dst, sem, at, target):
        copy = pltpu.make_async_remote_copy(
            src_ref=src, dst_ref=dst, send_sem=sem.at[(0,) + at], recv_sem=sem.at[(1,) + at],
            device_id=target, device_id_type=MESH,
        )
        copy.start()
        started.append(copy)
        return copy

    w[y, zh, c, :, 0:KEY] = wq[...]
    w[y, zh, c, :, KEY:] = wk[...]
    factor = jnp.exp(-rate[...]) * (1 - reset[...]).astype(F32)
    factor = jnp.concatenate([factor, jnp.zeros_like(factor)], axis=1)
    rt[zl, x] = jnp.broadcast_to(factor, rt.shape[2:])
    zr[:, pl.ds(zl, 1)] = jnp.zeros((zr.shape[0], 1) + zr.shape[2:], BF16)
    zi = zh * ZL + zl
    peers = [dev(x=(x + k) % X) for k in range(1, X)]
    peers += [dev(y=(y + k) % Y) for k in range(1, Y)]
    for k in range(1, ZL * ZH):
        zt = (zi + k) % (ZL * ZH)
        peers.append(dev(zl=zt % ZL, zh=zt // ZL))
    peers.append(dev(c=1 - c))
    barrier = pltpu.get_barrier_semaphore()
    for peer in peers:
        pl.semaphore_signal(barrier, inc=1, device_id=peer, device_id_type=MESH)
    pl.semaphore_wait(barrier, len(peers))

    mine = pl.ds(x * xs, xs)
    part = w.at[y, zh, c, mine]
    got = [send(part, part, a1, (k,), dev(zh=(zh + k) % ZH)) for k in range(1, ZH)]
    own = rt.at[zl, x]
    gotx = [send(own, own, rx, (k,), dev(x=(x + k) % X)) for k in range(1, X)]
    for copy in got:
        copy.wait_recv()
    part = w.at[y, :, c, mine]
    goty = [send(part, part, a2, (k,), dev(y=(y + k) % Y)) for k in range(1, Y)]
    arrived = [[] for _ in range(X)]
    for j in range(Y):
        if j:
            goty[j - 1].wait_recv()
        part = w.at[(y + Y - j) % Y, :, c, mine]
        for k in range(1, X):
            arrived[k].append(send(part, part, a3, (j, k), dev(x=(x + k) % X)))
    cores = []
    for k in range(X):
        for copy in arrived[k]:
            copy.wait_recv()
        part = w.at[:, :, c, pl.ds(((x + X - k) % X) * xs, xs)]
        cores.append(send(part, part, a4, (k,), dev(c=1 - c)))
    for copy in gotx:
        copy.wait_recv()
    own = rt.at[zl]
    gotz = [send(own, own, rz, (k,), dev(zl=(zl + k) % ZL)) for k in range(1, ZL)]
    for copy in cores:
        copy.wait_recv()

    both = dot(tok[...], w[...].reshape(width, 2 * KEY), 1, 0)
    low = jnp.exp(jnp.minimum(both, 0.0))
    features = jnp.where(both > 0, both + 1.0, low)
    slope[...] = jnp.where(both > 0, 1.0, low)
    feat[...] = features.astype(BF16)
    turned = features.T.astype(BF16)

    ins = []
    for j in range(CHUNKS):
        at = slice(j * X * wide, (j + 1) * X * wide)
        update = (dot(turned[KEY:], tok[:, at], 1, 0) / rows).astype(BF16)
        grad = dot(turned[:KEY], cot[:, at], 1, 0).astype(BF16)
        for q in range(X):
            sin[j, q, 0] = update[:, q * wide:(q + 1) * wide]
            sin[j, q, 1] = grad[:, q * wide:(q + 1) * wide]
        ins.append([
            send(sin.at[j, (x + k) % X], rin.at[j, x], s_in, (j, k), dev(x=(x + k) % X))
            for k in range(1, X)
        ])
        rin[j, x] = sin[j, x]

    eye = lax.broadcasted_iota(jnp.int32, (KEY, KEY), 0) == lax.broadcasted_iota(jnp.int32, (KEY, KEY), 1)

    def column(row):
        return jnp.sum(jnp.where(eye, row[0:1, :KEY], 0.0), axis=1, keepdims=True)

    for copy in gotz:
        copy.wait_recv()
    keep = [column(rt[zl, i]) for i in range(X)]
    whole = []
    for z in range(ZL):
        total = column(rt[z, 0])
        for i in range(1, X):
            total = total * column(rt[z, i])
        whole.append(total)
    ahead, behind = [], []
    for z in range(ZL):
        f = jnp.where(z < zl, jnp.ones_like(keep[0]), 0.0)
        for m in range(z + 1, ZL):
            f = f * jnp.where(m < zl, whole[m], 1.0)
        ahead.append(f)
        f = jnp.where(z > zl, jnp.ones_like(keep[0]), 0.0)
        for m in range(z):
            f = f * jnp.where(m > zl, whole[m], 1.0)
        behind.append(f)

    def totals(j):
        for copy in ins[j]:
            copy.wait_recv()
        forward = rin[j, 0, 0].astype(F32)
        backward = rin[j, X - 1, 1].astype(F32)
        for i in range(1, X):
            forward = keep[i] * forward + rin[j, i, 0].astype(F32)
            backward = keep[X - 1 - i] * backward + rin[j, X - 1 - i, 1].astype(F32)
        zs[j, 0] = forward.astype(BF16)
        zs[j, 1] = backward.astype(BF16)
        copies = []
        for k in range(1, ZL):
            zt = (zl + k) % ZL
            way = jnp.where(zt < zl, 1, 0)
            copies.append(send(zs.at[j, way], zr.at[j, zl], s_z, (j, k), dev(zl=zt)))
        return copies

    def finish(j, copies):
        for copy in copies:
            copy.wait_recv()
        forward = jnp.zeros((KEY, wide), F32)
        backward = jnp.zeros((KEY, wide), F32)
        for z in range(ZL):
            block = zr[j, z].astype(F32)
            forward = forward + ahead[z] * block
            backward = backward + behind[z] * block
        for i in range(X):
            sb[j, i, 0] = forward.astype(BF16)
            sb[j, X - 1 - i, 1] = backward.astype(BF16)
            if i < X - 1:
                forward = keep[i] * forward + rin[j, i, 0].astype(F32)
                backward = keep[X - 1 - i] * backward + rin[j, X - 1 - i, 1].astype(F32)
        back = [
            send(sb.at[j, (x + k) % X], read.at[j, x], s_bk, (j, k), dev(x=(x + k) % X))
            for k in range(1, X)
        ]
        read[j, x] = sb[j, x]
        return back

    backs = []
    pending = totals(0)
    for j in range(CHUNKS):
        following = totals(j + 1) if j + 1 < CHUNKS else None
        backs.append(finish(j, pending))
        pending = following

    read_grad = jnp.zeros((rows, KEY), F32)
    feature_grad = jnp.zeros((rows, KEY), F32)
    for j in range(CHUNKS):
        for copy in backs[j]:
            copy.wait_recv()
        for q in range(X):
            at = slice((j * X + q) * wide, (j * X + q + 1) * wide)
            read_grad = read_grad + dot(cot[:, at], read[j, q, 0], 1, 1)
            feature_grad = feature_grad + dot(tok[:, at], read[j, q, 1], 1, 1)
    bg[...] = (jnp.concatenate([read_grad, feature_grad / rows], axis=1) * slope[...]).astype(BF16)

    span = width // ZL
    per = span // (X * Y * ZH * C)
    pair = []
    for z in range(ZL):
        g = dot(tok[:, z * span:(z + 1) * span], bg[...], 0, 0)
        g = g.reshape(X * Y * ZH, C, per, 2 * KEY)
        first = g[:, 0].reshape(X, Y, ZH * per, 2 * KEY)
        second = g[:, 1].reshape(X, Y, ZH * per, 2 * KEY)
        gown[z] = jnp.where(c == 0, first, second)
        gsnd[z] = jnp.where(c == 0, second, first).astype(BF16)
        pair.append(send(gsnd.at[z], grcv.at[z], s_c, (z,), dev(c=1 - c)))
    first_x, first_y = [], []
    for z in range(ZL):
        pair[z].wait_recv()
        total = gown[z] + grcv[z].astype(F32)
        gown[z] = total
        hb[z] = total.astype(BF16)
        if z == half - 1:
            for k in range(1, X):
                xt = (x + k) % X
                first_x.append(send(hb.at[pl.ds(0, half), xt], r1a.at[k], e1a, (k,), dev(x=xt)))
    for k in range(1, Y):
        yt = (y + k) % Y
        first_y.append(send(hb.at[pl.ds(half, half), :, yt], r1b.at[k], e1b, (k,), dev(y=yt)))

    def outputs(j):
        for q in range(X):
            at = slice((j * X + q) * wide, (j * X + q + 1) * wide)
            out[:, at] = (tok[:, at].astype(F32) + dot(feat[:, :KEY], read[j, q, 0], 1, 0)).astype(BF16)

    def input_grads(j):
        for q in range(X):
            n = (j * X + q) * wide
            at = slice(n, n + wide)
            flat = w[...].reshape(width, 2 * KEY)
            total = cot[:, at].astype(F32) + dot(feat[:, KEY:], read[j, q, 1], 1, 0) / rows
            igrad[:, at] = (total + dot(bg[...], flat[n:n + wide], 1, 1)).astype(BF16)

    for j in range(CHUNKS):
        outputs(j)
    for copy in first_x:
        copy.wait_recv()
    total = gown[0:half, x]
    for k in range(1, X):
        total = total + r1a[k].astype(F32)
    acc1a[...] = total
    h1a[...] = total.astype(BF16)
    second_y = []
    for k in range(1, Y):
        yt = (y + k) % Y
        second_y.append(send(h1a.at[:, yt], r2a.at[k], e2a, (k,), dev(y=yt)))
    for copy in first_y:
        copy.wait_recv()
    total = gown[half:, :, y]
    for k in range(1, Y):
        total = total + r1b[k].astype(F32)
    acc1b[...] = total
    h1b[...] = total.astype(BF16)
    second_x = []
    for k in range(1, X):
        xt = (x + k) % X
        second_x.append(send(h1b.at[:, xt], r2b.at[k], e2b, (k,), dev(x=xt)))

    for j in range(CHUNKS // 2):
        input_grads(j)
    for copy in second_y:
        copy.wait_recv()
    total = acc1a[:, y]
    for k in range(1, Y):
        total = total + r2a[k].astype(F32)
    fin[0:half] = total.reshape(half, ZH, per, 2 * KEY)
    for copy in second_x:
        copy.wait_recv()
    total = acc1b[:, x]
    for k in range(1, X):
        total = total + r2b[k].astype(F32)
    fin[half:] = total.reshape(ZL - half, ZH, per, 2 * KEY)
    last = []
    for k in range(1, ZL * ZH):
        zt = (zi + k) % (ZL * ZH)
        last.append(send(fin.at[zt % ZL, zt // ZL], r3.at[k], e3, (k,), dev(zl=zt % ZL, zh=zt // ZL)))

    for j in range(CHUNKS // 2, CHUNKS):
        input_grads(j)
    for copy in last:
        copy.wait_recv()
    total = fin[zl, zh]
    for k in range(1, ZL * ZH):
        total = total + r3[k]
    gq[...] = total[:, :KEY]
    gk[...] = total[:, KEY:]

    for copy in started:
        copy.wait_send()


def local(tokens, cotangent, query_weight, key_weight, forget_rate, resets):
    rows, width = tokens.shape[2:]
    shard = query_weight.shape[0]
    wide = width // (CHUNKS * X)
    half = ZL // 2
    span = width // ZL
    per = span // (X * Y * ZH * C)
    lanes = 2 * KEY
    vm = pltpu.VMEM
    sem = pltpu.SemaphoreType.DMA
    scratch = [
        vm((Y, ZH, C, shard, lanes), BF16),
        vm((ZL, X, 8, lanes), F32),
        vm((CHUNKS, X, 2, KEY, wide), BF16),
        vm((CHUNKS, X, 2, KEY, wide), BF16),
        vm((CHUNKS, 2, KEY, wide), BF16),
        vm((CHUNKS, ZL, KEY, wide), BF16),
        vm((CHUNKS, X, 2, KEY, wide), BF16),
        vm((CHUNKS, X, 2, KEY, wide), BF16),
        vm((rows, lanes), BF16),
        vm((rows, lanes), F32),
        vm((rows, lanes), BF16),
        vm((ZL, X, Y, ZH * per, lanes), F32),
        vm((ZL, X, Y, ZH * per, lanes), BF16),
        vm((ZL, X, Y, ZH * per, lanes), BF16),
        vm((ZL, X, Y, ZH * per, lanes), BF16),
        vm((X, half, Y, ZH * per, lanes), BF16),
        vm((Y, half, X, ZH * per, lanes), BF16),
        vm((half, Y, ZH * per, lanes), F32),
        vm((half, X, ZH * per, lanes), F32),
        vm((half, Y, ZH * per, lanes), BF16),
        vm((half, X, ZH * per, lanes), BF16),
        vm((Y, half, ZH * per, lanes), BF16),
        vm((X, half, ZH * per, lanes), BF16),
        vm((ZL, ZH, per, lanes), F32),
        vm((ZL * ZH, per, lanes), F32),
        sem((2, ZH)), sem((2, Y)), sem((2, Y, X)), sem((2, X)), sem((2, X)), sem((2, ZL)),
        sem((2, CHUNKS, X)), sem((2, CHUNKS, ZL)), sem((2, CHUNKS, X)), sem((2, ZL)),
        sem((2, X)), sem((2, Y)), sem((2, Y)), sem((2, X)), sem((2, ZL * ZH)),
    ]
    whole = pl.BlockSpec(memory_space=pltpu.VMEM)
    output, input_grad, grad_query, grad_key = pl.pallas_call(
        body,
        out_shape=(
            jax.ShapeDtypeStruct((rows, width), BF16),
            jax.ShapeDtypeStruct((rows, width), BF16),
            jax.ShapeDtypeStruct((per, KEY), F32),
            jax.ShapeDtypeStruct((per, KEY), F32),
        ),
        in_specs=[whole] * 6,
        out_specs=(whole,) * 4,
        scratch_shapes=scratch,
        compiler_params=pltpu.CompilerParams(
            collective_id=0, has_side_effects=True, vmem_limit_bytes=48 * 1024 * 1024
        ),
        cost_estimate=pl.CostEstimate(
            flops=16 * rows * width * KEY, bytes_accessed=8 * rows * width, transcendentals=rows * lanes
        ),
    )(tokens[0, 0], cotangent[0, 0], query_weight, key_weight, forget_rate[0], resets)
    return output[None, None], input_grad[None, None], grad_query, grad_key


def solution(mesh):
    placed = (
        P("seg", "dp", None, None),
        P("seg", "dp", None, None),
        P("dp", None),
        P("dp", None),
        P("seg", "dp", None),
        P("seg", "dp"),
    )
    return jax.shard_map(
        local,
        mesh=mesh,
        in_specs=placed,
        out_specs=(
            P("seg", "dp", None, None),
            P("seg", "dp", None, None),
            P(("seg", "dp"), None),
            P(("seg", "dp"), None),
        ),
        check_vma=False,
    )
```

time: 985 us -> 89.1 us (0.09)
  waiting for transfers between devices: 863 us -> 0 us
  Pallas kernels: 0 us -> 80.5 us
  other arithmetic: 52 us -> 0 us
  blocking collectives: 37.5 us -> 0 us
  between operations: 14.6 us -> 1.32 us
  matrix products: 11.8 us -> 0 us
    unnamed x5 -> x0, waiting for transfers between devices: 469 us -> none
    all_gather x3 -> x0, waiting for transfers between devices: 394 us -> none  [the longest x2 313 us: prefix(): everything = jax.tree.map(lambda part: lax.all_gather(part, axis), array)]
    pallas_call x0 -> x1, Pallas kernels: none -> 80.5 us  [local(): pl.pallas_call(body, out_shape=(jax.ShapeDtypeStruct((rows, width), BF16)...]
    select_n x32 -> x0, other arithmetic: 50.6 us -> none  [step(): return jax.tree.map(lambda a, b: jnp.where(reached, a, b), new, before)]
    all_gather x1 -> x0, blocking collectives: 37.5 us -> none  [prefix(): everything = jax.tree.map(lambda part: lax.all_gather(part, axis), array)]
    dot_general x9 -> x0, matrix products: 11.8 us -> none  [the longest x1 1.97 us: local(): jnp.dot(columns, lax.all_gather(stacked, 'dp', axis=0, tiled=True), prefe...]
  transfers between devices with their start and end apart: 4 -> 0, of which waited for: 4 -> 0; matrix products, arithmetic and copies ran while one was open for 3% -> 0% of each run, Pallas kernels for 0% -> 0%
where the time goes in v1:
time: 89.1 us; the launch traced here: 88.8 us
  Pallas kernels  80.5 us (90%)
  local copies, waits for them, and re-layouts  7.06 us (8%)
  between operations  1.32 us (1%)
    pallas_call x1, Pallas kernels, local(): pl.pallas_call(body, out_shape=(jax.ShapeDtypeStruct((rows, width), BF16)...  80.5 us
    unnamed x14, local copies, waits for them, and re-layouts  7.06 us

profile of v1, /device:TPU:1, one launch (start us, length us, event | category | flops | bytes accessed | tf_op | source)
XLA Modules:
  0.0 88.8 jit_solution(15574168309786735804)
XLA Ops:
  1.3 0.0 copy-start.3
  1.3 0.8 copy.10.wq
  2.1 0.0 copy-done.3
  2.1 0.0 copy-start.2
  2.1 0.1 copy.11.wk
  2.3 0.5 copy-done.2
  2.8 0.0 copy-start
  2.8 1.2 %copy-done = bf16[1,1,128,4096]{3,2,1,0:T(8,128)(2,1)S(1)} copy-done((bf16[1,1,128,4096]{3,2,1,0:T(8,128)(2,1)S(1)}, bf16[1,1,128,4096]{3,2,1,0:T(8,128)(2,1)}, u32[]{:S(2)}) %copy-start) | copy-done | bytes 1048600
  4.0 0.0 copy-start.1
  4.0 1.2 %copy-done.1 = bf16[1,1,128,4096]{3,2,1,0:T(8,128)(2,1)S(1)} copy-done((bf16[1,1,128,4096]{3,2,1,0:T(8,128)(2,1)S(1)}, bf16[1,1,128,4096]{3,2,1,0:T(8,128)(2,1)}, u32[]{:S(2)}) %copy-start.1) | copy-done | bytes 1048600
  5.2 80.5 %shard_map.93 = (bf16[128,4096]{1,0:T(8,128)(2,1)S(1)}, bf16[128,4096]{1,0:T(8,128)(2,1)S(1)}, f32[8,64]{1,0:T(8,128)S(1)}, f32[8,64]{1,0:T(8,128)S(1)}) custom-call(bf16[128,4096]{1,0:T(8,128)(2,1)S(1)} %bitcast.7, bf16[128,4096]{1,0:T(8,128)(2,1)S(1)} %bitcast.8, bf16[128,64]{1,0:T(8,128)(2,1)S(1)} %copy.10.wq, bf16[128,64]{1,0:T(8,128)(2,1)S(1)} %copy.11.wk, ...), custom_call_target="tpu_custom_call" | custom-call | flops 536870912 | bytes 4194304 | tf_op jit(solution)/shard_map/pallas_call | solution.py:339
  85.7 1.0 %copy.17 = bf16[1,1,128,4096]{3,2,1,0:T(8,128)(2,1)} copy(bf16[1,1,128,4096]{3,2,1,0:T(8,128)(2,1)S(1)} %bitcast.6) | data formatting | bytes 2097152
  86.7 1.0 %copy.18 = bf16[1,1,128,4096]{3,2,1,0:T(8,128)(2,1)} copy(bf16[1,1,128,4096]{3,2,1,0:T(8,128)(2,1)S(1)} %bitcast.5) | data formatting | bytes 2097152
  87.7 0.6 copy.19
  88.3 0.6 copy.20
Async XLA Ops:
  1.3 0.8 copy-start.3
  2.1 0.7 copy-start.2
  2.8 1.2 %copy-start = (bf16[1,1,128,4096]{3,2,1,0:T(8,128)(2,1)S(1)}, bf16[1,1,128,4096]{3,2,1,0:T(8,128)(2,1)}, u32[]{:S(2)}) copy-start(bf16[1,1,128,4096]{3,2,1,0:T(8,128)(2,1)} %param.6) | copy-start | bytes 3145732
  4.0 1.2 %copy-start.1 = (bf16[1,1,128,4096]{3,2,1,0:T(8,128)(2,1)S(1)}, bf16[1,1,128,4096]{3,2,1,0:T(8,128)(2,1)}, u32[]{:S(2)}) copy-start(bf16[1,1,128,4096]{3,2,1,0:T(8,128)(2,1)} %param.7) | copy-start | bytes 3145732

commit v2 on v0

v2 whole, which is shorter than its diff:
```python
import jax
import jax.numpy as jnp
from jax import lax
from jax.experimental import pallas as pl
from jax.experimental.pallas import tpu as pltpu
from jax.sharding import PartitionSpec as P

ZL, X = 4, 4
Y, ZH, C = 4, 4, 2
CHUNKS = 4
KEY = 64
VMEM_LIMIT = 56 * 1024 * 1024
F32 = jnp.float32
BF16 = jnp.bfloat16
MESH = pl.DeviceIdType.MESH
QUERY, WRITE = 0, 1
FORE, BACK = 0, 1


def dot(a, b, ca, cb):
    return lax.dot_general(a, b, (((ca,), (cb,)), ((), ())), preferred_element_type=F32)


def feature(values):
    return jnp.where(values > 0, values + 1.0, jnp.exp(jnp.minimum(values, 0.0)))


def feature_slope(values):
    return jnp.where(values > 0, 1.0, jnp.exp(jnp.minimum(values, 0.0)))


def body(
    tok_in, cot_in, wq, wk, rate, reset,
    out, igrad, gq, gk,
    tok, cot, tokt, w, rt, sin, rin, zt, zs, zm, za, zb, sb, read, feat, slope, bg,
    gown, gsnd, grcv, hb, r1, fin, r3,
    s_l, s_zs, s_zr, s_y, s_w, s_rx, s_rz, s_in, s_a, s_bs, s_br, s_bk, s_c, s_xy, s_e,
):
    rows, width = tok.shape
    shard = wq.shape[1]
    wide = width // (CHUNKS * X)
    nz = ZL * ZH
    reach = (ZH - 1) * ZL // 2
    s = lax.axis_index("seg")
    b = lax.axis_index("dp")
    zl, x = s // X, s % X
    y, zh, c = b // (ZH * C), (b // C) % ZH, b % C
    zi = zh * ZL + zl

    def dev(zl=zl, x=x, y=y, zh=zh, c=c):
        return (zl * X + x, (y * ZH + zh) * C + c)

    started = []

    def make(src, dst, send_sem, recv_sem, target):
        return pltpu.make_async_remote_copy(
            src_ref=src, dst_ref=dst, send_sem=send_sem, recv_sem=recv_sem,
            device_id=target, device_id_type=MESH,
        )

    def send(src, dst, sem, at, target):
        copy = make(src, dst, sem.at[(0,) + at], sem.at[(1,) + at], target)
        copy.start()
        started.append(copy)
        return copy

    load_tok = pltpu.make_async_copy(tok_in, tok, s_l.at[0])
    load_cot = pltpu.make_async_copy(cot_in, cot, s_l.at[1])
    load_tok.start()
    load_cot.start()
    lanes = pl.ds(pl.multiple_of(c * shard, shard), shard)
    w[QUERY, y, zh, :, lanes] = wq[...]
    w[WRITE, y, zh, :, lanes] = wk[...]
    factor = jnp.exp(-rate[...]) * (1 - reset[...]).astype(F32)
    factor = jnp.concatenate([factor, jnp.zeros_like(factor)], axis=1)
    rt[zl, x] = jnp.broadcast_to(factor, rt.shape[2:])
    za[...] = jnp.zeros_like(za)
    zb[...] = jnp.zeros_like(zb)
    peers = [dev(c=1 - c)]
    peers += [dev(x=(x + k) % X) for k in range(1, X)]
    peers += [dev(y=(y + k) % Y) for k in range(1, Y)]
    peers += [dev(zl=(zl + k) % ZL) for k in range(1, ZL)]
    near = len(peers)
    for o in range(1, ZH):
        peers.append(dev(zl=jnp.where(o * ZL - zl <= reach, 0, ZL - 1), zh=(zh + o) % ZH))
    edge = (zl == 0) | (zl == ZL - 1)
    barrier = pltpu.get_barrier_semaphore()
    for peer in peers:
        pl.semaphore_signal(barrier, inc=1, device_id=peer, device_id_type=MESH)
    pl.semaphore_wait(barrier, near + jnp.where(edge, reach, 0))

    def block(part, o):
        return w.at[part, y, (zh + o) % ZH, :, lanes]

    spread = []
    for part in (WRITE, QUERY):
        for d in range(1, reach + 1):
            zt_ = (zi + jnp.where(zl == 0, -d, d) + nz) % nz
            o = (d - 1) // ZL + 1
            o = jnp.where(zl == 0, o, ZH - o)
            spread.append(make(
                block(part, 0), block(part, 0), s_zs.at[part, d], s_zr.at[part, o],
                dev(zl=zt_ % ZL, zh=zt_ // ZL),
            ))

    @pl.when(edge)
    def _():
        for copy in spread:
            copy.start()

    def arrive_z(part, o):
        make(block(part, o), block(part, o), s_zs.at[part, 0], s_zr.at[part, o], dev(zh=(zh + 1) % ZH)).wait_recv()

    along_y = {}

    def start_y(part, o):
        along_y[part, o] = [
            send(block(part, o), block(part, o), s_y, (part, o, k), dev(y=(y + k) % Y)) for k in range(1, Y)
        ]

    to_core = {WRITE: [], QUERY: []}

    def start_core(part, o):
        for copy in along_y[part, o]:
            copy.wait_recv()
        column = w.at[part, :, (zh + o) % ZH, :, lanes]
        to_core[part].append(send(column, column, s_w, (part, o), dev(c=1 - c)))

    offsets = sorted(range(1, ZH), key=lambda o: min(o, ZH - o))
    start_y(WRITE, 0)
    own = rt.at[zl, x]
    gotx = [send(own, own, s_rx, (k,), dev(x=(x + k) % X)) for k in range(1, X)]
    load_tok.wait()
    step = width // 8
    for n in range(8):
        tokt[n * step:(n + 1) * step] = tok[:, n * step:(n + 1) * step].T
    for copy in gotx:
        copy.wait_recv()
    own = rt.at[zl]
    gotz = [send(own, own, s_rz, (k,), dev(zl=(zl + k) % ZL)) for k in range(1, ZL)]
    load_cot.wait()
    for o in offsets:
        arrive_z(WRITE, o)
        start_y(WRITE, o)
    start_y(QUERY, 0)
    start_core(WRITE, 0)
    for o in offsets:
        arrive_z(QUERY, o)
        start_y(QUERY, o)
        start_core(WRITE, o)
    for copy in to_core[WRITE]:
        copy.wait_recv()

    pairs = [(n // ZH, n % ZH, slice(n * C * shard, (n + 1) * C * shard)) for n in range(Y * ZH)]

    def turned(part):
        total = jnp.zeros((KEY, rows), F32)
        for i, j, at in pairs:
            total = total + dot(w[part, i, j], tok[:, at], 1, 1)
        return feature(total).astype(BF16)

    def straight(part):
        total = jnp.zeros((rows, KEY), F32)
        for i, j, at in pairs:
            total = total + dot(tok[:, at], w[part, i, j], 1, 1)
        feat[part] = feature(total).astype(BF16)
        slope[part] = feature_slope(total)

    ins = {}

    def exchange(way, weights, values, scale):
        for j in range(CHUNKS):
            at = slice(j * X * wide, (j + 1) * X * wide)
            term = (dot(weights, values[:, at], 1, 0) * scale).astype(BF16)
            for q in range(X):
                sin[way, j, q] = term[:, q * wide:(q + 1) * wide]
            ins[way, j] = [
                send(sin.at[way, j, (x + k) % X], rin.at[way, j, x], s_in, (way, j, k), dev(x=(x + k) % X))
                for k in range(1, X)
            ]
            rin[way, j, x] = sin[way, j, x]

    exchange(FORE, turned(WRITE), tok, 1.0 / rows)
    for o in [0] + offsets:
        start_core(QUERY, o)
    for copy in to_core[QUERY]:
        copy.wait_recv()
    exchange(BACK, turned(QUERY), cot, 1.0)

    eye = lax.broadcasted_iota(jnp.int32, (KEY, KEY), 0) == lax.broadcasted_iota(jnp.int32, (KEY, KEY), 1)

    def column(row):
        return jnp.sum(jnp.where(eye, row[0:1, :KEY], 0.0), axis=1, keepdims=True)

    for copy in gotz:
        copy.wait_recv()
    keep = [column(rt[zl, i]) for i in range(X)]
    whole = keep[0]
    for i in range(1, X):
        whole = whole * keep[i]
    place = {FORE: zl, BACK: ZL - 1 - zl}
    ahead = {FORE: 1, BACK: -1}
    order = {FORE: list(range(X)), BACK: list(range(X))[::-1]}
    from_a, from_b = {}, {}
    for way, row in ((FORE, ZL - 2), (BACK, 1)):
        skipped = column(rt[row, 0])
        for i in range(1, X):
            skipped = skipped * column(rt[row, i])
        one = jnp.ones_like(skipped)
        p = place[way]
        from_a[way] = jnp.where(p % 2 == 1, one, 0.0)
        from_b[way] = jnp.where(p == 2, one, jnp.where(p == 3, skipped, 0.0))

    later = []

    def hop(way, steps):
        return dev(zl=(zl + ahead[way] * steps + ZL) % ZL)

    def pass_a(way, j):
        return make(zs.at[way, j], za.at[way, j], s_a.at[0, way, j], s_a.at[1, way, j], hop(way, 1))

    def pass_b(way, j, n):
        return make(zm.at[way, j], zb.at[way, j], s_bs.at[way, j, n], s_br.at[way, j], hop(way, n))

    def totals(way, j):
        for copy in ins[way, j]:
            copy.wait_recv()
        total = rin[way, j, order[way][0]].astype(F32)
        for i in order[way][1:]:
            total = keep[i] * total + rin[way, j, i].astype(F32)
        zt[way, j] = total
        zs[way, j] = total.astype(BF16)

        @pl.when(place[way] % 2 == 0)
        def _():
            pass_a(way, j).start()

    def relay(way, j):
        @pl.when(place[way] == 1)
        def _():
            pass_a(way, j).wait_recv()
            zm[way, j] = (whole * za[way, j].astype(F32) + zt[way, j]).astype(BF16)
            pass_b(way, j, 1).start()
            pass_b(way, j, 2).start()

    backs = {}

    def finish(way, j):
        @pl.when(place[way] >= 2)
        def _():
            pass_b(way, j, 1).wait_recv()

        @pl.when(place[way] == 3)
        def _():
            pass_a(way, j).wait_recv()

        state = from_a[way] * za[way, j].astype(F32) + from_b[way] * zb[way, j].astype(F32)
        for n, i in enumerate(order[way]):
            sb[way, j, i] = state.astype(BF16)
            if n < X - 1:
                state = keep[i] * state + rin[way, j, i].astype(F32)
        backs[way, j] = [
            send(sb.at[way, j, (x + k) % X], read.at[way, j, x], s_bk, (way, j, k), dev(x=(x + k) % X))
            for k in range(1, X)
        ]
        read[way, j, x] = sb[way, j, x]

    plan = [(way, j) for way in (FORE, BACK) for j in range(CHUNKS)]
    for n in range(len(plan) + 2):
        if n < len(plan):
            totals(*plan[n])
        if 1 <= n <= len(plan):
            relay(*plan[n - 1])
        if n >= 2:
            finish(*plan[n - 2])
    straight(QUERY)
    straight(WRITE)

    half = ZL // 2
    span = width // ZL
    per = span // (X * Y * ZH * C)
    blank = jnp.zeros((rows, KEY), BF16)
    pair, plane = {}, {}

    def against(way, values, js):
        total = jnp.zeros((rows, KEY), F32)
        for j in js:
            for copy in backs[way, j]:
                copy.wait_recv()
            for q in range(X):
                at = slice((j * X + q) * wide, (j * X + q + 1) * wide)
                total = total + dot(values[:, at], read[way, j, q], 1, 1)
        return total

    def product(part, grad):
        low = jnp.concatenate([grad, blank], axis=1)
        high = jnp.concatenate([blank, grad], axis=1)
        for z in range(half):
            g = dot(tokt[z * span:(z + 1) * span], low, 1, 0)
            g = g + dot(tokt[(z + half) * span:(z + half + 1) * span], high, 1, 0)
            g = g.reshape(X * Y * ZH, C, per, 2 * KEY)
            first = g[:, 0].reshape(X, Y, ZH * per, 2 * KEY)
            second = g[:, 1].reshape(X, Y, ZH * per, 2 * KEY)
            gown[part, z] = jnp.where(c == 0, first, second)
            gsnd[part, z] = jnp.where(c == 0, second, first).astype(BF16)
            pair[part, z] = send(gsnd.at[part, z], grcv.at[part, z], s_c, (part, z), dev(c=1 - c))

    def over_plane(part):
        for z in range(half):
            pair[part, z].wait_recv()
            total = gown[part, z] + grcv[part, z].astype(F32)
            gown[part, z] = total
            hb[part, z] = total.astype(BF16)
        plane[part] = []
        for k in range(1, X * Y):
            xt, yt = (x + k // Y) % X, (y + k % Y) % Y
            plane[part].append(send(hb.at[part, :, xt, yt], r1.at[part, k], s_xy, (part, k), dev(x=xt, y=yt)))

    def gather_plane(part):
        for copy in plane[part]:
            copy.wait_recv()
        total = gown[part, :, x, y]
        for k in range(1, X * Y):
            total = total + r1[part, k].astype(F32)
        for h in range(2):
            piece = total[:, :, h * KEY:(h + 1) * KEY].reshape(half, ZH, per, KEY)
            fin[h * half:(h + 1) * half, :, :, part * KEY:(part + 1) * KEY] = piece

    query_grad = (against(FORE, cot, range(CHUNKS)) * slope[QUERY]).astype(BF16)
    bg[QUERY] = query_grad
    product(QUERY, query_grad)
    wanted = against(BACK, tok, range(CHUNKS - 1))
    over_plane(QUERY)
    wanted = wanted + against(BACK, tok, range(CHUNKS - 1, CHUNKS))
    key_grad = (wanted / rows * slope[WRITE]).astype(BF16)
    bg[WRITE] = key_grad
    product(WRITE, key_grad)
    over_plane(WRITE)

    for j in range(CHUNKS):
        for q in range(X):
            at = slice((j * X + q) * wide, (j * X + q + 1) * wide)
            out[:, at] = (tok[:, at].astype(F32) + dot(feat[QUERY], read[FORE, j, q], 1, 0)).astype(BF16)
    gather_plane(QUERY)
    gather_plane(WRITE)
    last = []
    for k in range(1, nz):
        zt_ = (zi + k) % nz
        last.append(send(fin.at[zt_ % ZL, zt_ // ZL], r3.at[k], s_e, (k,), dev(zl=zt_ % ZL, zh=zt_ // ZL)))

    for j in range(CHUNKS):
        for q in range(X):
            n = (j * X + q) * wide
            at = slice(n, n + wide)
            i, m, n = n // (ZH * C * shard), n // (C * shard) % ZH, n % (C * shard)
            total = cot[:, at].astype(F32) + dot(feat[WRITE], read[BACK, j, q], 1, 0) / rows
            for part in (QUERY, WRITE):
                total = total + dot(bg[part], w[part, i, m, :, n:n + wide], 1, 0)
            igrad[:, at] = total.astype(BF16)
    for copy in last:
        copy.wait_recv()
    total = fin[zl, zh]
    for k in range(1, nz):
        total = total + r3[k]
    gq[...] = total[:, :KEY]
    gk[...] = total[:, KEY:]

    for copy in started:
        copy.wait_send()

    @pl.when(edge)
    def _():
        for copy in spread:
            copy.wait_send()

    for way, j in plan:
        @pl.when(place[way] % 2 == 0)
        def _():
            pass_a(way, j).wait_send()

        @pl.when(place[way] == 1)
        def _():
            pass_b(way, j, 1).wait_send()
            pass_b(way, j, 2).wait_send()


def publish(*refs):
    n = len(refs) // 3
    sem = refs[-1]
    inward = [pltpu.make_async_copy(refs[i], refs[2 * n + i], sem.at[0, i]) for i in range(n)]
    outward = [pltpu.make_async_copy(refs[2 * n + i], refs[n + i], sem.at[1, i]) for i in range(n)]
    for copy in inward:
        copy.start()
    for i in range(n):
        inward[i].wait()
        outward[i].start()
    for copy in outward:
        copy.wait()


def local(tokens, cotangent, query_weight, key_weight, forget_rate, resets):
    rows, width = tokens.shape[2:]
    shard = query_weight.shape[0]
    wide = width // (CHUNKS * X)
    half = ZL // 2
    span = width // ZL
    per = span // (X * Y * ZH * C)
    nz = ZL * ZH
    reach = (ZH - 1) * ZL // 2
    lanes = 2 * KEY
    vm = pltpu.VMEM
    sem = pltpu.SemaphoreType.DMA
    scratch = [
        vm((rows, width), BF16),
        vm((rows, width), BF16),
        vm((width, rows), BF16),
        vm((2, Y, ZH, KEY, C * shard), BF16),
        vm((ZL, X, 8, lanes), F32),
        vm((2, CHUNKS, X, KEY, wide), BF16),
        vm((2, CHUNKS, X, KEY, wide), BF16),
        vm((2, CHUNKS, KEY, wide), F32),
        vm((2, CHUNKS, KEY, wide), BF16),
        vm((2, CHUNKS, KEY, wide), BF16),
        vm((2, CHUNKS, KEY, wide), BF16),
        vm((2, CHUNKS, KEY, wide), BF16),
        vm((2, CHUNKS, X, KEY, wide), BF16),
        vm((2, CHUNKS, X, KEY, wide), BF16),
        vm((2, rows, KEY), BF16),
        vm((2, rows, KEY), F32),
        vm((2, rows, KEY), BF16),
        vm((2, half, X, Y, ZH * per, lanes), F32),
        vm((2, half, X, Y, ZH * per, lanes), BF16),
        vm((2, half, X, Y, ZH * per, lanes), BF16),
        vm((2, half, X, Y, ZH * per, lanes), BF16),
        vm((2, X * Y, half, ZH * per, lanes), BF16),
        vm((ZL, ZH, per, lanes), F32),
        vm((nz, per, lanes), F32),
        sem((2,)), sem((2, reach + 1)), sem((2, ZH)), sem((2, 2, ZH, Y)), sem((2, 2, ZH)),
        sem((2, X)), sem((2, ZL)), sem((2, 2, CHUNKS, X)), sem((2, 2, CHUNKS)),
        sem((2, CHUNKS, 3)), sem((2, CHUNKS)), sem((2, 2, CHUNKS, X)), sem((2, 2, half)),
        sem((2, 2, X * Y)), sem((2, nz)),
    ]
    whole = pl.BlockSpec(memory_space=pltpu.VMEM)
    anywhere = pl.BlockSpec(memory_space=pl.ANY)
    shapes = (
        jax.ShapeDtypeStruct((rows, width), BF16),
        jax.ShapeDtypeStruct((rows, width), BF16),
        jax.ShapeDtypeStruct((per, KEY), F32),
        jax.ShapeDtypeStruct((per, KEY), F32),
    )
    results = pl.pallas_call(
        body,
        out_shape=shapes,
        in_specs=[anywhere] * 2 + [whole] * 4,
        out_specs=(whole,) * 4,
        scratch_shapes=scratch,
        compiler_params=pltpu.CompilerParams(
            collective_id=0, has_side_effects=True, vmem_limit_bytes=VMEM_LIMIT
        ),
        cost_estimate=pl.CostEstimate(
            flops=16 * rows * width * KEY, bytes_accessed=8 * rows * width, transcendentals=rows * lanes
        ),
    )(tokens[0, 0], cotangent[0, 0], query_weight.T, key_weight.T, forget_rate[0], resets)
    output, input_grad, grad_query, grad_key = pl.pallas_call(
        publish,
        out_shape=shapes,
        in_specs=[anywhere] * 4,
        out_specs=(anywhere,) * 4,
        scratch_shapes=[vm(r.shape, r.dtype) for r in shapes] + [sem((2, 4))],
        compiler_params=pltpu.CompilerParams(vmem_limit_bytes=VMEM_LIMIT),
    )(*results)
    return output[None, None], input_grad[None, None], grad_query, grad_key


def solution(mesh):
    placed = (
        P("seg", "dp", None, None),
        P("seg", "dp", None, None),
        P("dp", None),
        P("dp", None),
        P("seg", "dp", None),
        P("seg", "dp"),
    )
    return jax.shard_map(
        local,
        mesh=mesh,
        in_specs=placed,
        out_specs=(
            P("seg", "dp", None, None),
            P("seg", "dp", None, None),
            P(("seg", "dp"), None),
            P(("seg", "dp"), None),
        ),
        check_vma=False,
    )
```

time: 985 us -> 83.2 us (0.08)
  waiting for transfers between devices: 863 us -> 0 us
  Pallas kernels: 0 us -> 81.7 us
  other arithmetic: 52 us -> 0 us
  blocking collectives: 37.5 us -> 0 us
  between operations: 14.6 us -> 1.29 us
  matrix products: 11.8 us -> 0 us
    unnamed x5 -> x0, waiting for transfers between devices: 469 us -> none
    all_gather x3 -> x0, waiting for transfers between devices: 394 us -> none  [the longest x2 313 us: prefix(): everything = jax.tree.map(lambda part: lax.all_gather(part, axis), array)]
    pallas_call x0 -> x2, Pallas kernels: none -> 81.7 us  [the longest x1 79.1 us: local(): pl.pallas_call(body, out_shape=shapes, in_specs=[anywhere] * 2 + [whole]...]
    select_n x32 -> x0, other arithmetic: 50.6 us -> none  [step(): return jax.tree.map(lambda a, b: jnp.where(reached, a, b), new, before)]
    all_gather x1 -> x0, blocking collectives: 37.5 us -> none  [prefix(): everything = jax.tree.map(lambda part: lax.all_gather(part, axis), array)]
    dot_general x9 -> x0, matrix products: 11.8 us -> none  [the longest x1 1.97 us: local(): jnp.dot(columns, lax.all_gather(stacked, 'dp', axis=0, tiled=True), prefe...]
  transfers between devices with their start and end apart: 4 -> 0, of which waited for: 4 -> 0; matrix products, arithmetic and copies ran while one was open for 3% -> 0% of each run, Pallas kernels for 0% -> 0%
where the time goes in v2:
time: 83.2 us; the launch traced here: 83 us
  Pallas kernels  81.7 us (98%)
  between operations  1.29 us (2%)
    pallas_call x1, Pallas kernels, local(): pl.pallas_call(body, out_shape=shapes, in_specs=[anywhere] * 2 + [whole]...  79.1 us
    pallas_call x1, Pallas kernels, local(): pl.pallas_call(publish, out_shape=shapes, in_specs=[anywhere] * 4, out_sp...  2.61 us

profile of v2, /device:TPU:1, one launch (start us, length us, event | category | flops | bytes accessed | tf_op | source)
XLA Modules:
  0.0 83.0 jit_solution(9866959985165053933)
XLA Ops:
  1.3 79.1 %shard_map.93 = (bf16[128,4096]{1,0:T(8,128)(2,1)}, bf16[128,4096]{1,0:T(8,128)(2,1)}, f32[8,64]{1,0:T(8,128)}, f32[8,64]{1,0:T(8,128)}) custom-call(bf16[128,4096]{1,0:T(8,128)(2,1)} %bitcast.7, bf16[128,4096]{1,0:T(8,128)(2,1)} %bitcast.8, bf16[64,128]{1,0:T(8,128)(2,1)} %bitcast.9, bf16[64,128]{1,0:T(8,128)(2,1)} %bitcast.10, f32[1,64]{1,0:T(1,128)} %bitcast.11, ...), custom_call_target="tpu_custom_call" | custom-call | flops 536870912 | bytes 4194304 | tf_op jit(solution)/shard_map/pallas_call | solution.py:451
  80.4 2.6 %shard_map.94 = (bf16[128,4096]{1,0:T(8,128)(2,1)}, bf16[128,4096]{1,0:T(8,128)(2,1)}, f32[8,64]{1,0:T(8,128)}, f32[8,64]{1,0:T(8,128)}) custom-call(bf16[128,4096]{1,0:T(8,128)(2,1)} %get-tuple-element.12.refs_0_, bf16[128,4096]{1,0:T(8,128)(2,1)} %get-tuple-element.13.refs_1_, f32[8,64]{1,0:T(8,128)} %get-tuple-element.14.refs_2_, ...), custom_call_target="tpu_custom_call" | custom-call | tf_op jit(solution)/shard_map/pallas_call | solution.py:464

commit v3 on v2

--- a/solution.py
+++ b/solution.py
@@ -9,6 +9,7 @@
 Y, ZH, C = 4, 4, 2
 CHUNKS = 4
 KEY = 64
+PIECES = 4
 VMEM_LIMIT = 56 * 1024 * 1024
 F32 = jnp.float32
 BF16 = jnp.bfloat16
@@ -30,11 +31,11 @@
 
 
 def body(
-    tok_in, cot_in, wq, wk, rate, reset,
-    out, igrad, gq, gk,
-    tok, cot, tokt, w, rt, sin, rin, zt, zs, zm, za, zb, sb, read, feat, slope, bg,
+    tok_in, cot_in, wq_in, wk_in, rate_in, reset_in,
+    out_to, igrad_to, gq_to, gk_to,
+    tok, cot, wq, wk, rate, reset, out, igrad, gq, gk, tokt, w, rt, sin, rin, zt, zs, zm, za, zb, sb, read, feat, slope, bg,
     gown, gsnd, grcv, hb, r1, fin, r3,
-    s_l, s_zs, s_zr, s_y, s_w, s_rx, s_rz, s_in, s_a, s_bs, s_br, s_bk, s_c, s_xy, s_e,
+    s_l, s_s, s_zs, s_zr, s_y, s_w, s_rx, s_rz, s_in, s_a, s_bs, s_br, s_bk, s_c, s_xy, s_e,
 ):
     rows, width = tok.shape
     shard = wq.shape[1]
@@ -64,16 +65,10 @@
         started.append(copy)
         return copy
 
-    load_tok = pltpu.make_async_copy(tok_in, tok, s_l.at[0])
-    load_cot = pltpu.make_async_copy(cot_in, cot, s_l.at[1])
-    load_tok.start()
-    load_cot.start()
-    lanes = pl.ds(pl.multiple_of(c * shard, shard), shard)
-    w[QUERY, y, zh, :, lanes] = wq[...]
-    w[WRITE, y, zh, :, lanes] = wk[...]
-    factor = jnp.exp(-rate[...]) * (1 - reset[...]).astype(F32)
-    factor = jnp.concatenate([factor, jnp.zeros_like(factor)], axis=1)
-    rt[zl, x] = jnp.broadcast_to(factor, rt.shape[2:])
+    moves = ((wk_in, wk), (wq_in, wq), (rate_in, rate), (reset_in, reset), (tok_in, tok), (cot_in, cot))
+    loads = [pltpu.make_async_copy(src, dst, s_l.at[i]) for i, (src, dst) in enumerate(moves)]
+    for copy in loads:
+        copy.start()
     za[...] = jnp.zeros_like(za)
     zb[...] = jnp.zeros_like(zb)
     peers = [dev(c=1 - c)]
@@ -87,6 +82,14 @@
     barrier = pltpu.get_barrier_semaphore()
     for peer in peers:
         pl.semaphore_signal(barrier, inc=1, device_id=peer, device_id_type=MESH)
+    for copy in loads[:4]:
+        copy.wait()
+    lanes = pl.ds(pl.multiple_of(c * shard, shard), shard)
+    w[QUERY, y, zh, :, lanes] = wq[...]
+    w[WRITE, y, zh, :, lanes] = wk[...]
+    factor = jnp.exp(-rate[...]) * (1 - reset[...]).astype(F32)
+    factor = jnp.concatenate([factor, jnp.zeros_like(factor)], axis=1)
+    rt[zl, x] = jnp.broadcast_to(factor, rt.shape[2:])
     pl.semaphore_wait(barrier, near + jnp.where(edge, reach, 0))
 
     def block(part, o):
@@ -94,7 +97,7 @@
 
     spread = []
     for part in (WRITE, QUERY):
-        for d in range(1, reach + 1):
+        for d in range(reach, 0, -1):
             zt_ = (zi + jnp.where(zl == 0, -d, d) + nz) % nz
             o = (d - 1) // ZL + 1
             o = jnp.where(zl == 0, o, ZH - o)
@@ -130,7 +133,7 @@
     start_y(WRITE, 0)
     own = rt.at[zl, x]
     gotx = [send(own, own, s_rx, (k,), dev(x=(x + k) % X)) for k in range(1, X)]
-    load_tok.wait()
+    loads[4].wait()
     step = width // 8
     for n in range(8):
         tokt[n * step:(n + 1) * step] = tok[:, n * step:(n + 1) * step].T
@@ -138,7 +141,7 @@
         copy.wait_recv()
     own = rt.at[zl]
     gotz = [send(own, own, s_rz, (k,), dev(zl=(zl + k) % ZL)) for k in range(1, ZL)]
-    load_cot.wait()
+    loads[5].wait()
     for o in offsets:
         arrive_z(WRITE, o)
         start_y(WRITE, o)
@@ -181,11 +184,13 @@
             rin[way, j, x] = sin[way, j, x]
 
     exchange(FORE, turned(WRITE), tok, 1.0 / rows)
+    straight(WRITE)
     for o in [0] + offsets:
         start_core(QUERY, o)
     for copy in to_core[QUERY]:
         copy.wait_recv()
     exchange(BACK, turned(QUERY), cot, 1.0)
+    straight(QUERY)
 
     eye = lax.broadcasted_iota(jnp.int32, (KEY, KEY), 0) == lax.broadcasted_iota(jnp.int32, (KEY, KEY), 1)
 
@@ -273,8 +278,6 @@
             relay(*plan[n - 1])
         if n >= 2:
             finish(*plan[n - 2])
-    straight(QUERY)
-    straight(WRITE)
 
     half = ZL // 2
     span = width // ZL
@@ -312,7 +315,7 @@
             gown[part, z] = total
             hb[part, z] = total.astype(BF16)
         plane[part] = []
-        for k in range(1, X * Y):
+        for k in sorted(range(1, X * Y), key=lambda k: -min(k // Y, X - k // Y) - min(k % Y, Y - k % Y)):
             xt, yt = (x + k // Y) % X, (y + k % Y) % Y
             plane[part].append(send(hb.at[part, :, xt, yt], r1.at[part, k], s_xy, (part, k), dev(x=xt, y=yt)))
 
@@ -341,10 +344,12 @@
         for q in range(X):
             at = slice((j * X + q) * wide, (j * X + q + 1) * wide)
             out[:, at] = (tok[:, at].astype(F32) + dot(feat[QUERY], read[FORE, j, q], 1, 0)).astype(BF16)
+    stores = [pltpu.make_async_copy(out, out_to, s_s.at[0])]
+    stores[0].start()
     gather_plane(QUERY)
     gather_plane(WRITE)
     last = []
-    for k in range(1, nz):
+    for k in sorted(range(1, nz), key=lambda k: -min(k, nz - k)):
         zt_ = (zi + k) % nz
         last.append(send(fin.at[zt_ % ZL, zt_ // ZL], r3.at[k], s_e, (k,), dev(zl=zt_ % ZL, zh=zt_ // ZL)))
 
@@ -357,6 +362,8 @@
             for part in (QUERY, WRITE):
                 total = total + dot(bg[part], w[part, i, m, :, n:n + wide], 1, 0)
             igrad[:, at] = total.astype(BF16)
+    stores.append(pltpu.make_async_copy(igrad, igrad_to, s_s.at[1]))
+    stores[1].start()
     for copy in last:
         copy.wait_recv()
     total = fin[zl, zh]
@@ -364,7 +371,12 @@
         total = total + r3[k]
     gq[...] = total[:, :KEY]
     gk[...] = total[:, KEY:]
-
+    for i, (src, dst) in enumerate(((gq, gq_to), (gk, gk_to))):
+        stores.append(pltpu.make_async_copy(src, dst, s_s.at[2 + i]))
+        stores[-1].start()
+
+    for copy in stores:
+        copy.wait()
     for copy in started:
         copy.wait_send()
 
@@ -385,15 +397,20 @@
 
 
 def publish(*refs):
-    n = len(refs) // 3
     sem = refs[-1]
-    inward = [pltpu.make_async_copy(refs[i], refs[2 * n + i], sem.at[0, i]) for i in range(n)]
-    outward = [pltpu.make_async_copy(refs[2 * n + i], refs[n + i], sem.at[1, i]) for i in range(n)]
-    for copy in inward:
-        copy.start()
-    for i in range(n):
-        inward[i].wait()
-        outward[i].start()
+    pieces = []
+    for src, dst, held in zip(refs[:4], refs[4:8], refs[8:12]):
+        n = PIECES if src.shape[0] % (16 * PIECES) == 0 else 1
+        m = src.shape[0] // n
+        pieces += [tuple(ref.at[pl.ds(i * m, m)] for ref in (src, held, dst)) for i in range(n)]
+    inward, outward = [], []
+    for i, (src, held, dst) in enumerate(pieces):
+        inward.append(pltpu.make_async_copy(src, held, sem.at[0, i]))
+        outward.append(pltpu.make_async_copy(held, dst, sem.at[1, i]))
+        inward[-1].start()
+    for copy, following in zip(inward, outward):
+        copy.wait()
+        following.start()
     for copy in outward:
         copy.wait()
 
@@ -413,6 +430,14 @@
     scratch = [
         vm((rows, width), BF16),
         vm((rows, width), BF16),
+        vm((KEY, shard), BF16),
+        vm((KEY, shard), BF16),
+        vm((1, KEY), F32),
+        vm((1, 1), jnp.int32),
+        vm((rows, width), BF16),
+        vm((rows, width), BF16),
+        vm((per, KEY), F32),
+        vm((per, KEY), F32),
         vm((width, rows), BF16),
         vm((2, Y, ZH, KEY, C * shard), BF16),
         vm((ZL, X, 8, lanes), F32),
@@ -435,12 +460,11 @@
         vm((2, X * Y, half, ZH * per, lanes), BF16),
         vm((ZL, ZH, per, lanes), F32),
         vm((nz, per, lanes), F32),
-        sem((2,)), sem((2, reach + 1)), sem((2, ZH)), sem((2, 2, ZH, Y)), sem((2, 2, ZH)),
+        sem((6,)), sem((4,)), sem((2, reach + 1)), sem((2, ZH)), sem((2, 2, ZH, Y)), sem((2, 2, ZH)),
         sem((2, X)), sem((2, ZL)), sem((2, 2, CHUNKS, X)), sem((2, 2, CHUNKS)),
         sem((2, CHUNKS, 3)), sem((2, CHUNKS)), sem((2, 2, CHUNKS, X)), sem((2, 2, half)),
         sem((2, 2, X * Y)), sem((2, nz)),
     ]
-    whole = pl.BlockSpec(memory_space=pltpu.VMEM)
     anywhere = pl.BlockSpec(memory_space=pl.ANY)
     shapes = (
         jax.ShapeDtypeStruct((rows, width), BF16),
@@ -451,8 +475,8 @@
     results = pl.pallas_call(
         body,
         out_shape=shapes,
-        in_specs=[anywhere] * 2 + [whole] * 4,
-        out_specs=(whole,) * 4,
+        in_specs=[anywhere] * 6,
+        out_specs=(anywhere,) * 4,
         scratch_shapes=scratch,
         compiler_params=pltpu.CompilerParams(
             collective_id=0, has_side_effects=True, vmem_limit_bytes=VMEM_LIMIT
@@ -466,7 +490,7 @@
         out_shape=shapes,
         in_specs=[anywhere] * 4,
         out_specs=(anywhere,) * 4,
-        scratch_shapes=[vm(r.shape, r.dtype) for r in shapes] + [sem((2, 4))],
+        scratch_shapes=[vm(r.shape, r.dtype) for r in shapes] + [sem((2, 2 * PIECES + 2))],
         compiler_params=pltpu.CompilerParams(vmem_limit_bytes=VMEM_LIMIT),
     )(*results)
     return output[None, None], input_grad[None, None], grad_query, grad_key

time: 83.2 us -> 78.8 us (0.947)
  Pallas kernels: 81.7 us -> 77.4 us
    pallas_call x1, Pallas kernels: 79.1 us -> 74.9 us  [local(): pl.pallas_call(body, out_shape=shapes, in_specs=[anywhere] * 6, out_specs...]
where the time goes in v3:
time: 78.8 us; the launch traced here: 78.7 us
  Pallas kernels  77.4 us (98%)
  between operations  1.29 us (2%)
    pallas_call x1, Pallas kernels, local(): pl.pallas_call(body, out_shape=shapes, in_specs=[anywhere] * 6, out_specs...  74.9 us
    pallas_call x1, Pallas kernels, local(): pl.pallas_call(publish, out_shape=shapes, in_specs=[anywhere] * 4, out_sp...  2.44 us

profile of v3, /device:TPU:1, one launch (start us, length us, event | category | flops | bytes accessed | tf_op | source)
XLA Modules:
  0.0 78.7 jit_solution(2933327701338110621)
XLA Ops:
  1.3 74.9 %shard_map.93 = (bf16[128,4096]{1,0:T(8,128)(2,1)}, bf16[128,4096]{1,0:T(8,128)(2,1)}, f32[8,64]{1,0:T(8,128)}, f32[8,64]{1,0:T(8,128)}) custom-call(bf16[128,4096]{1,0:T(8,128)(2,1)} %bitcast.7, bf16[128,4096]{1,0:T(8,128)(2,1)} %bitcast.8, bf16[64,128]{1,0:T(8,128)(2,1)} %bitcast.9, bf16[64,128]{1,0:T(8,128)(2,1)} %bitcast.10, f32[1,64]{1,0:T(1,128)} %bitcast.11, ...), custom_call_target="tpu_custom_call" | custom-call | flops 536870912 | bytes 4194304 | tf_op jit(solution)/shard_map/pallas_call | solution.py:475
  76.2 2.4 %shard_map.94 = (bf16[128,4096]{1,0:T(8,128)(2,1)}, bf16[128,4096]{1,0:T(8,128)(2,1)}, f32[8,64]{1,0:T(8,128)}, f32[8,64]{1,0:T(8,128)}) custom-call(bf16[128,4096]{1,0:T(8,128)(2,1)} %get-tuple-element.12.refs_0_, bf16[128,4096]{1,0:T(8,128)(2,1)} %get-tuple-element.13.refs_1_, f32[8,64]{1,0:T(8,128)} %get-tuple-element.14.refs_2_, ...), custom_call_target="tpu_custom_call" | custom-call | tf_op jit(solution)/shard_map/pallas_call | solution.py:488

commit v4 on v3

--- a/solution.py
+++ b/solution.py
@@ -7,9 +7,8 @@
 
 ZL, X = 4, 4
 Y, ZH, C = 4, 4, 2
-CHUNKS = 4
+CHUNKS = 2
 KEY = 64
-PIECES = 4
 VMEM_LIMIT = 56 * 1024 * 1024
 F32 = jnp.float32
 BF16 = jnp.bfloat16
@@ -32,14 +31,15 @@
 
 def body(
     tok_in, cot_in, wq_in, wk_in, rate_in, reset_in,
-    out_to, igrad_to, gq_to, gk_to,
-    tok, cot, wq, wk, rate, reset, out, igrad, gq, gk, tokt, w, rt, sin, rin, zt, zs, zm, za, zb, sb, read, feat, slope, bg,
+    out, igrad, gq, gk,
+    tok, cot, wq, wk, rate, reset, tokt, w, rt, sin, rin, zt, zs, zm, za, zb, sb, read, feat, slope, bg,
     gown, gsnd, grcv, hb, r1, fin, r3,
-    s_l, s_s, s_zs, s_zr, s_y, s_w, s_rx, s_rz, s_in, s_a, s_bs, s_br, s_bk, s_c, s_xy, s_e,
+    s_l, s_zs, s_zr, s_y, s_w, s_rx, s_rz, s_in, s_a, s_bs, s_br, s_bk, s_c, s_xy, s_e,
 ):
     rows, width = tok.shape
     shard = wq.shape[1]
     wide = width // (CHUNKS * X)
+    block_width = min(wide, C * shard)
     nz = ZL * ZH
     reach = (ZH - 1) * ZL // 2
     s = lax.axis_index("seg")
@@ -80,7 +80,7 @@
         peers.append(dev(zl=jnp.where(o * ZL - zl <= reach, 0, ZL - 1), zh=(zh + o) % ZH))
     edge = (zl == 0) | (zl == ZL - 1)
     barrier = pltpu.get_barrier_semaphore()
-    for peer in peers:
+    for peer in peers[::-1]:
         pl.semaphore_signal(barrier, inc=1, device_id=peer, device_id_type=MESH)
     for copy in loads[:4]:
         copy.wait()
@@ -121,13 +121,36 @@
             send(block(part, o), block(part, o), s_y, (part, o, k), dev(y=(y + k) % Y)) for k in range(1, Y)
         ]
 
-    to_core = {WRITE: [], QUERY: []}
+    to_core = {WRITE: []}
 
     def start_core(part, o):
         for copy in along_y[part, o]:
             copy.wait_recv()
         column = w.at[part, :, (zh + o) % ZH, :, lanes]
         to_core[part].append(send(column, column, s_w, (part, o), dev(c=1 - c)))
+
+    def left():
+        for copy in started:
+            copy.wait_send()
+        started.clear()
+
+    def left_early():
+        left()
+
+        @pl.when(edge)
+        def _():
+            for copy in spread:
+                copy.wait_send()
+
+        for way, j in plan:
+            @pl.when(place[way] % 2 == 0)
+            def _():
+                pass_a(way, j).wait_send()
+
+            @pl.when(place[way] == 1)
+            def _():
+                pass_b(way, j, 1).wait_send()
+                pass_b(way, j, 2).wait_send()
 
     offsets = sorted(range(1, ZH), key=lambda o: min(o, ZH - o))
     start_y(WRITE, 0)
@@ -145,12 +168,12 @@
     for o in offsets:
         arrive_z(WRITE, o)
         start_y(WRITE, o)
-    start_y(QUERY, 0)
-    start_core(WRITE, 0)
+    for o in [0] + offsets:
+        start_core(WRITE, o)
     for o in offsets:
         arrive_z(QUERY, o)
-        start_y(QUERY, o)
-        start_core(WRITE, o)
+    line = w.at[QUERY, y, :, :, lanes]
+    queries_y = [send(line, line, s_y, (QUERY, 0, k), dev(y=(y + k) % Y)) for k in range(1, Y)]
     for copy in to_core[WRITE]:
         copy.wait_recv()
 
@@ -185,10 +208,10 @@
 
     exchange(FORE, turned(WRITE), tok, 1.0 / rows)
     straight(WRITE)
-    for o in [0] + offsets:
-        start_core(QUERY, o)
-    for copy in to_core[QUERY]:
+    for copy in queries_y:
         copy.wait_recv()
+    column = w.at[QUERY, :, :, :, lanes]
+    send(column, column, s_w, (QUERY, 0), dev(c=1 - c)).wait_recv()
     exchange(BACK, turned(QUERY), cot, 1.0)
     straight(QUERY)
 
@@ -344,8 +367,10 @@
         for q in range(X):
             at = slice((j * X + q) * wide, (j * X + q + 1) * wide)
             out[:, at] = (tok[:, at].astype(F32) + dot(feat[QUERY], read[FORE, j, q], 1, 0)).astype(BF16)
-    stores = [pltpu.make_async_copy(out, out_to, s_s.at[0])]
-    stores[0].start()
+    early = started[:]
+    started[:] = [copy for copy in early if not any(copy is other for part in plane for other in plane[part])]
+    kept = [copy for copy in early if not any(copy is other for other in started)]
+    left_early()
     gather_plane(QUERY)
     gather_plane(WRITE)
     last = []
@@ -353,17 +378,16 @@
         zt_ = (zi + k) % nz
         last.append(send(fin.at[zt_ % ZL, zt_ // ZL], r3.at[k], s_e, (k,), dev(zl=zt_ % ZL, zh=zt_ // ZL)))
 
-    for j in range(CHUNKS):
-        for q in range(X):
-            n = (j * X + q) * wide
-            at = slice(n, n + wide)
-            i, m, n = n // (ZH * C * shard), n // (C * shard) % ZH, n % (C * shard)
-            total = cot[:, at].astype(F32) + dot(feat[WRITE], read[BACK, j, q], 1, 0) / rows
-            for part in (QUERY, WRITE):
-                total = total + dot(bg[part], w[part, i, m, :, n:n + wide], 1, 0)
-            igrad[:, at] = total.astype(BF16)
-    stores.append(pltpu.make_async_copy(igrad, igrad_to, s_s.at[1]))
-    stores[1].start()
+    for n in range(0, width, block_width):
+        at = slice(n, n + block_width)
+        j, q, k = n // (X * wide), n // wide % X, n % wide
+        i, m, n = n // (ZH * C * shard), n // (C * shard) % ZH, n % (C * shard)
+        total = cot[:, at].astype(F32) + dot(feat[WRITE], read[BACK, j, q, :, k:k + block_width], 1, 0) / rows
+        for part in (QUERY, WRITE):
+            total = total + dot(bg[part], w[part, i, m, :, n:n + block_width], 1, 0)
+        igrad[:, at] = total.astype(BF16)
+    for copy in kept:
+        copy.wait_send()
     for copy in last:
         copy.wait_recv()
     total = fin[zl, zh]
@@ -371,47 +395,15 @@
         total = total + r3[k]
     gq[...] = total[:, :KEY]
     gk[...] = total[:, KEY:]
-    for i, (src, dst) in enumerate(((gq, gq_to), (gk, gk_to))):
-        stores.append(pltpu.make_async_copy(src, dst, s_s.at[2 + i]))
-        stores[-1].start()
-
-    for copy in stores:
-        copy.wait()
-    for copy in started:
-        copy.wait_send()
-
-    @pl.when(edge)
-    def _():
-        for copy in spread:
-            copy.wait_send()
-
-    for way, j in plan:
-        @pl.when(place[way] % 2 == 0)
-        def _():
-            pass_a(way, j).wait_send()
-
-        @pl.when(place[way] == 1)
-        def _():
-            pass_b(way, j, 1).wait_send()
-            pass_b(way, j, 2).wait_send()
+
+    left()
 
 
 def publish(*refs):
-    sem = refs[-1]
-    pieces = []
-    for src, dst, held in zip(refs[:4], refs[4:8], refs[8:12]):
-        n = PIECES if src.shape[0] % (16 * PIECES) == 0 else 1
-        m = src.shape[0] // n
-        pieces += [tuple(ref.at[pl.ds(i * m, m)] for ref in (src, held, dst)) for i in range(n)]
-    inward, outward = [], []
-    for i, (src, held, dst) in enumerate(pieces):
-        inward.append(pltpu.make_async_copy(src, held, sem.at[0, i]))
-        outward.append(pltpu.make_async_copy(held, dst, sem.at[1, i]))
-        inward[-1].start()
-    for copy, following in zip(inward, outward):
-        copy.wait()
-        following.start()
-    for copy in outward:
+    copies = [pltpu.make_async_copy(refs[i], refs[4 + i], refs[8].at[i]) for i in range(4)]
+    for copy in copies:
+        copy.start()
+    for copy in copies:
         copy.wait()
 
 
@@ -434,10 +426,6 @@
         vm((KEY, shard), BF16),
         vm((1, KEY), F32),
         vm((1, 1), jnp.int32),
-        vm((rows, width), BF16),
-        vm((rows, width), BF16),
-        vm((per, KEY), F32),
-        vm((per, KEY), F32),
         vm((width, rows), BF16),
         vm((2, Y, ZH, KEY, C * shard), BF16),
         vm((ZL, X, 8, lanes), F32),
@@ -460,12 +448,13 @@
         vm((2, X * Y, half, ZH * per, lanes), BF16),
         vm((ZL, ZH, per, lanes), F32),
         vm((nz, per, lanes), F32),
-        sem((6,)), sem((4,)), sem((2, reach + 1)), sem((2, ZH)), sem((2, 2, ZH, Y)), sem((2, 2, ZH)),
+        sem((6,)), sem((2, reach + 1)), sem((2, ZH)), sem((2, 2, ZH, Y)), sem((2, 2, ZH)),
         sem((2, X)), sem((2, ZL)), sem((2, 2, CHUNKS, X)), sem((2, 2, CHUNKS)),
         sem((2, CHUNKS, 3)), sem((2, CHUNKS)), sem((2, 2, CHUNKS, X)), sem((2, 2, half)),
         sem((2, 2, X * Y)), sem((2, nz)),
     ]
     anywhere = pl.BlockSpec(memory_space=pl.ANY)
+    whole = pl.BlockSpec(memory_space=pltpu.VMEM)
     shapes = (
         jax.ShapeDtypeStruct((rows, width), BF16),
         jax.ShapeDtypeStruct((rows, width), BF16),
@@ -474,9 +463,9 @@
     )
     results = pl.pallas_call(
         body,
-        out_shape=shapes,
+        out_shape=tuple(vm(r.shape, r.dtype) for r in shapes),
         in_specs=[anywhere] * 6,
-        out_specs=(anywhere,) * 4,
+        out_specs=(whole,) * 4,
         scratch_shapes=scratch,
         compiler_params=pltpu.CompilerParams(
             collective_id=0, has_side_effects=True, vmem_limit_bytes=VMEM_LIMIT
@@ -490,8 +479,7 @@
         out_shape=shapes,
         in_specs=[anywhere] * 4,
         out_specs=(anywhere,) * 4,
-        scratch_shapes=[vm(r.shape, r.dtype) for r in shapes] + [sem((2, 2 * PIECES + 2))],
-        compiler_params=pltpu.CompilerParams(vmem_limit_bytes=VMEM_LIMIT),
+        scratch_shapes=[sem((4,))], compiler_params=pltpu.CompilerParams(vmem_limit_bytes=16 * 1024 * 1024),
     )(*results)
     return output[None, None], input_grad[None, None], grad_query, grad_key
 

time: 78.8 us -> 76.1 us (0.966)
  Pallas kernels: 77.4 us -> 74.6 us
    pallas_call x1, Pallas kernels: 74.9 us -> 73.3 us  [local(): pl.pallas_call(body, out_shape=tuple((vm(r.shape, r.dtype) for r in shape...]
    pallas_call x1, Pallas kernels: 2.44 us -> 1.36 us  [local(): pl.pallas_call(publish, out_shape=shapes, in_specs=[anywhere] * 4, out_sp...]
where the time goes in v4:
time: 76.1 us; the launch traced here: 75.9 us
  Pallas kernels  74.6 us (98%)
  between operations  1.29 us (2%)
    pallas_call x1, Pallas kernels, local(): pl.pallas_call(body, out_shape=tuple((vm(r.shape, r.dtype) for r in shape...  73.3 us

profile of v4, /device:TPU:1, one launch (start us, length us, event | category | flops | bytes accessed | tf_op | source)
XLA Modules:
  0.0 75.9 jit_solution(17933713366191584020)
XLA Ops:
  1.3 73.3 %shard_map.93 = (bf16[128,4096]{1,0:T(8,128)(2,1)S(1)}, bf16[128,4096]{1,0:T(8,128)(2,1)S(1)}, f32[8,64]{1,0:T(8,128)S(1)}, f32[8,64]{1,0:T(8,128)S(1)}) custom-call(bf16[128,4096]{1,0:T(8,128)(2,1)} %bitcast.7, bf16[128,4096]{1,0:T(8,128)(2,1)} %bitcast.8, bf16[64,128]{1,0:T(8,128)(2,1)} %bitcast.9, bf16[64,128]{1,0:T(8,128)(2,1)} %bitcast.10, ...), custom_call_target="tpu_custom_call" | custom-call | flops 536870912 | bytes 4194304 | tf_op jit(solution)/shard_map/pallas_call | solution.py:464
  74.6 1.4 %shard_map.94 = (bf16[128,4096]{1,0:T(8,128)(2,1)}, bf16[128,4096]{1,0:T(8,128)(2,1)}, f32[8,64]{1,0:T(8,128)}, f32[8,64]{1,0:T(8,128)}) custom-call(bf16[128,4096]{1,0:T(8,128)(2,1)S(1)} %get-tuple-element.12.refs_0_, bf16[128,4096]{1,0:T(8,128)(2,1)S(1)} %get-tuple-element.13.refs_1_, f32[8,64]{1,0:T(8,128)S(1)} %get-tuple-element.14.refs_2_, ...), custom_call_target="tpu_custom_call" | custom-call | tf_op jit(solution)/shard_map/pallas_call | solution.py:477

commit v5 on v4

--- a/solution.py
+++ b/solution.py
@@ -32,13 +32,15 @@
 def body(
     tok_in, cot_in, wq_in, wk_in, rate_in, reset_in,
     out, igrad, gq, gk,
-    tok, cot, wq, wk, rate, reset, tokt, w, rt, sin, rin, zt, zs, zm, za, zb, sb, read, feat, slope, bg,
-    gown, gsnd, grcv, hb, r1, fin, r3,
-    s_l, s_zs, s_zr, s_y, s_w, s_rx, s_rz, s_in, s_a, s_bs, s_br, s_bk, s_c, s_xy, s_e,
+    tok, cot, wq, wk, rate, reset, tt, tsend, w, rt, sin, rin, zt, zs, zm, za, zb, sb, read, feat, slope, bg, bgs,
+    gown, hb, r1, fin, r3,
+    s_l, s_zs, s_zr, s_y, s_w, s_rx, s_rz, s_in, s_a, s_bs, s_br, s_bk, s_c, s_t, s_xy, s_e,
 ):
     rows, width = tok.shape
     shard = wq.shape[1]
     wide = width // (CHUNKS * X)
+    span = width // (ZL * C)
+    per = span // (X * Y * ZH)
     block_width = min(wide, C * shard)
     nz = ZL * ZH
     reach = (ZH - 1) * ZL // 2
@@ -118,7 +120,8 @@
 
     def start_y(part, o):
         along_y[part, o] = [
-            send(block(part, o), block(part, o), s_y, (part, o, k), dev(y=(y + k) % Y)) for k in range(1, Y)
+            send(block(part, o), block(part, o), s_y, (part, o, k), dev(y=(y + k) % Y))
+            for k in sorted(range(1, Y), key=lambda k: -min(k, Y - k))
         ]
 
     to_core = {WRITE: []}
@@ -159,7 +162,13 @@
     loads[4].wait()
     step = width // 8
     for n in range(8):
-        tokt[n * step:(n + 1) * step] = tok[:, n * step:(n + 1) * step].T
+        piece = tok[:, n * step:(n + 1) * step].astype(F32).T.reshape(step // (C * per), C, per, rows)
+        first = piece[:, 0].reshape(step // C, rows)
+        second = piece[:, 1].reshape(step // C, rows)
+        at = slice(n * step // C, (n + 1) * step // C)
+        tt[at, :rows] = jnp.where(c == 0, first, second).astype(BF16)
+        tsend[at] = jnp.where(c == 0, second, first).astype(BF16)
+    got_tokens = send(tsend, tt.at[:, pl.ds(rows, rows)], s_t, (), dev(c=1 - c))
     for copy in gotx:
         copy.wait_recv()
     own = rt.at[zl]
@@ -202,18 +211,12 @@
                 sin[way, j, q] = term[:, q * wide:(q + 1) * wide]
             ins[way, j] = [
                 send(sin.at[way, j, (x + k) % X], rin.at[way, j, x], s_in, (way, j, k), dev(x=(x + k) % X))
-                for k in range(1, X)
+                for k in sorted(range(1, X), key=lambda k: -min(k, X - k))
             ]
             rin[way, j, x] = sin[way, j, x]
 
     exchange(FORE, turned(WRITE), tok, 1.0 / rows)
     straight(WRITE)
-    for copy in queries_y:
-        copy.wait_recv()
-    column = w.at[QUERY, :, :, :, lanes]
-    send(column, column, s_w, (QUERY, 0), dev(c=1 - c)).wait_recv()
-    exchange(BACK, turned(QUERY), cot, 1.0)
-    straight(QUERY)
 
     eye = lax.broadcasted_iota(jnp.int32, (KEY, KEY), 0) == lax.broadcasted_iota(jnp.int32, (KEY, KEY), 1)
 
@@ -239,7 +242,12 @@
         from_a[way] = jnp.where(p % 2 == 1, one, 0.0)
         from_b[way] = jnp.where(p == 2, one, jnp.where(p == 3, skipped, 0.0))
 
-    later = []
+    for copy in queries_y:
+        copy.wait_recv()
+    column = w.at[QUERY, :, :, :, lanes]
+    send(column, column, s_w, (QUERY, 0), dev(c=1 - c)).wait_recv()
+    exchange(BACK, turned(QUERY), cot, 1.0)
+
 
     def hop(way, steps):
         return dev(zl=(zl + ahead[way] * steps + ZL) % ZL)
@@ -289,7 +297,7 @@
                 state = keep[i] * state + rin[way, j, i].astype(F32)
         backs[way, j] = [
             send(sb.at[way, j, (x + k) % X], read.at[way, j, x], s_bk, (way, j, k), dev(x=(x + k) % X))
-            for k in range(1, X)
+            for k in sorted(range(1, X), key=lambda k: -min(k, X - k))
         ]
         read[way, j, x] = sb[way, j, x]
 
@@ -301,12 +309,12 @@
             relay(*plan[n - 1])
         if n >= 2:
             finish(*plan[n - 2])
+    straight(QUERY)
 
     half = ZL // 2
-    span = width // ZL
-    per = span // (X * Y * ZH * C)
-    blank = jnp.zeros((rows, KEY), BF16)
-    pair, plane = {}, {}
+    blank = jnp.zeros((C * rows, KEY), BF16)
+    other, plane = {}, {}
+    got_tokens.wait_recv()
 
     def against(way, values, js):
         total = jnp.zeros((rows, KEY), F32)
@@ -318,25 +326,21 @@
                 total = total + dot(values[:, at], read[way, j, q], 1, 1)
         return total
 
-    def product(part, grad):
-        low = jnp.concatenate([grad, blank], axis=1)
-        high = jnp.concatenate([blank, grad], axis=1)
+    def share(part, grad):
+        bg[part] = grad
+        other[part] = send(bg.at[part], bgs.at[part], s_c, (part,), dev(c=1 - c))
+
+    def over_plane(part):
+        other[part].wait_recv()
+        grads = jnp.concatenate([bg[part], bgs[part]], axis=0)
+        low = jnp.concatenate([grads, blank], axis=1)
+        high = jnp.concatenate([blank, grads], axis=1)
         for z in range(half):
-            g = dot(tokt[z * span:(z + 1) * span], low, 1, 0)
-            g = g + dot(tokt[(z + half) * span:(z + half + 1) * span], high, 1, 0)
-            g = g.reshape(X * Y * ZH, C, per, 2 * KEY)
-            first = g[:, 0].reshape(X, Y, ZH * per, 2 * KEY)
-            second = g[:, 1].reshape(X, Y, ZH * per, 2 * KEY)
-            gown[part, z] = jnp.where(c == 0, first, second)
-            gsnd[part, z] = jnp.where(c == 0, second, first).astype(BF16)
-            pair[part, z] = send(gsnd.at[part, z], grcv.at[part, z], s_c, (part, z), dev(c=1 - c))
-
-    def over_plane(part):
-        for z in range(half):
-            pair[part, z].wait_recv()
-            total = gown[part, z] + grcv[part, z].astype(F32)
-            gown[part, z] = total
-            hb[part, z] = total.astype(BF16)
+            g = dot(tt[z * span:(z + 1) * span], low, 1, 0)
+            g = g + dot(tt[(z + half) * span:(z + half + 1) * span], high, 1, 0)
+            g = g.reshape(X, Y, ZH * per, 2 * KEY)
+            gown[part, z] = g
+            hb[part, z] = g.astype(BF16)
         plane[part] = []
         for k in sorted(range(1, X * Y), key=lambda k: -min(k // Y, X - k // Y) - min(k % Y, Y - k % Y)):
             xt, yt = (x + k // Y) % X, (y + k % Y) % Y
@@ -353,14 +357,12 @@
             fin[h * half:(h + 1) * half, :, :, part * KEY:(part + 1) * KEY] = piece
 
     query_grad = (against(FORE, cot, range(CHUNKS)) * slope[QUERY]).astype(BF16)
-    bg[QUERY] = query_grad
-    product(QUERY, query_grad)
+    share(QUERY, query_grad)
     wanted = against(BACK, tok, range(CHUNKS - 1))
     over_plane(QUERY)
     wanted = wanted + against(BACK, tok, range(CHUNKS - 1, CHUNKS))
     key_grad = (wanted / rows * slope[WRITE]).astype(BF16)
-    bg[WRITE] = key_grad
-    product(WRITE, key_grad)
+    share(WRITE, key_grad)
     over_plane(WRITE)
 
     for j in range(CHUNKS):
@@ -426,7 +428,8 @@
         vm((KEY, shard), BF16),
         vm((1, KEY), F32),
         vm((1, 1), jnp.int32),
-        vm((width, rows), BF16),
+        vm((width // C, C * rows), BF16),
+        vm((width // C, rows), BF16),
         vm((2, Y, ZH, KEY, C * shard), BF16),
         vm((ZL, X, 8, lanes), F32),
         vm((2, CHUNKS, X, KEY, wide), BF16),
@@ -441,17 +444,16 @@
         vm((2, rows, KEY), BF16),
         vm((2, rows, KEY), F32),
         vm((2, rows, KEY), BF16),
+        vm((2, rows, KEY), BF16),
         vm((2, half, X, Y, ZH * per, lanes), F32),
-        vm((2, half, X, Y, ZH * per, lanes), BF16),
-        vm((2, half, X, Y, ZH * per, lanes), BF16),
         vm((2, half, X, Y, ZH * per, lanes), BF16),
         vm((2, X * Y, half, ZH * per, lanes), BF16),
         vm((ZL, ZH, per, lanes), F32),
         vm((nz, per, lanes), F32),
         sem((6,)), sem((2, reach + 1)), sem((2, ZH)), sem((2, 2, ZH, Y)), sem((2, 2, ZH)),
         sem((2, X)), sem((2, ZL)), sem((2, 2, CHUNKS, X)), sem((2, 2, CHUNKS)),
-        sem((2, CHUNKS, 3)), sem((2, CHUNKS)), sem((2, 2, CHUNKS, X)), sem((2, 2, half)),
-        sem((2, 2, X * Y)), sem((2, nz)),
+        sem((2, CHUNKS, 3)), sem((2, CHUNKS)), sem((2, 2, CHUNKS, X)), sem((2, 2)),
+        sem((2,)), sem((2, 2, X * Y)), sem((2, nz)),
     ]
     anywhere = pl.BlockSpec(memory_space=pl.ANY)
     whole = pl.BlockSpec(memory_space=pltpu.VMEM)

time: 76.1 us -> 75.1 us (0.987)
  Pallas kernels: 74.6 us -> 73.6 us
    pallas_call x1, Pallas kernels: 73.3 us -> 72.2 us  [local(): pl.pallas_call(body, out_shape=tuple((vm(r.shape, r.dtype) for r in shape...]
where the time goes in v5:
time: 75.1 us; the launch traced here: 74.9 us
  Pallas kernels  73.6 us (98%)
  between operations  1.29 us (2%)
    pallas_call x1, Pallas kernels, local(): pl.pallas_call(body, out_shape=tuple((vm(r.shape, r.dtype) for r in shape...  72.2 us

profile of v5, /device:TPU:1, one launch (start us, length us, event | category | flops | bytes accessed | tf_op | source)
XLA Modules:
  0.0 74.9 jit_solution(14423724059568026315)
XLA Ops:
  1.3 72.2 %shard_map.93 = (bf16[128,4096]{1,0:T(8,128)(2,1)S(1)}, bf16[128,4096]{1,0:T(8,128)(2,1)S(1)}, f32[8,64]{1,0:T(8,128)S(1)}, f32[8,64]{1,0:T(8,128)S(1)}) custom-call(bf16[128,4096]{1,0:T(8,128)(2,1)} %bitcast.7, bf16[128,4096]{1,0:T(8,128)(2,1)} %bitcast.8, bf16[64,128]{1,0:T(8,128)(2,1)} %bitcast.9, bf16[64,128]{1,0:T(8,128)(2,1)} %bitcast.10, ...), custom_call_target="tpu_custom_call" | custom-call | flops 536870912 | bytes 4194304 | tf_op jit(solution)/shard_map/pallas_call | solution.py:466
  73.5 1.4 %shard_map.94 = (bf16[128,4096]{1,0:T(8,128)(2,1)}, bf16[128,4096]{1,0:T(8,128)(2,1)}, f32[8,64]{1,0:T(8,128)}, f32[8,64]{1,0:T(8,128)}) custom-call(bf16[128,4096]{1,0:T(8,128)(2,1)S(1)} %get-tuple-element.12.refs_0_, bf16[128,4096]{1,0:T(8,128)(2,1)S(1)} %get-tuple-element.13.refs_1_, f32[8,64]{1,0:T(8,128)S(1)} %get-tuple-element.14.refs_2_, ...), custom_call_target="tpu_custom_call" | custom-call | tf_op jit(solution)/shard_map/pallas_call | solution.py:479

commit v6 on v5

--- a/solution.py
+++ b/solution.py
@@ -358,8 +358,8 @@
 
     query_grad = (against(FORE, cot, range(CHUNKS)) * slope[QUERY]).astype(BF16)
     share(QUERY, query_grad)
+    over_plane(QUERY)
     wanted = against(BACK, tok, range(CHUNKS - 1))
-    over_plane(QUERY)
     wanted = wanted + against(BACK, tok, range(CHUNKS - 1, CHUNKS))
     key_grad = (wanted / rows * slope[WRITE]).astype(BF16)
     share(WRITE, key_grad)

time: 75.1 us -> 75.2 us (level)
  no operation moved by 1% of the time
where the time goes in v6:
time: 75.2 us; the launch traced here: 75 us
  Pallas kernels  73.7 us (98%)
  between operations  1.29 us (2%)
    pallas_call x1, Pallas kernels, local(): pl.pallas_call(body, out_shape=tuple((vm(r.shape, r.dtype) for r in shape...  72.3 us

profile of v6, /device:TPU:1, one launch (start us, length us, event | category | flops | bytes accessed | tf_op | source)
XLA Modules:
  0.0 75.0 jit_solution(3739921505461448516)
XLA Ops:
  1.3 72.3 %shard_map.93 = (bf16[128,4096]{1,0:T(8,128)(2,1)S(1)}, bf16[128,4096]{1,0:T(8,128)(2,1)S(1)}, f32[8,64]{1,0:T(8,128)S(1)}, f32[8,64]{1,0:T(8,128)S(1)}) custom-call(bf16[128,4096]{1,0:T(8,128)(2,1)} %bitcast.7, bf16[128,4096]{1,0:T(8,128)(2,1)} %bitcast.8, bf16[64,128]{1,0:T(8,128)(2,1)} %bitcast.9, bf16[64,128]{1,0:T(8,128)(2,1)} %bitcast.10, ...), custom_call_target="tpu_custom_call" | custom-call | flops 536870912 | bytes 4194304 | tf_op jit(solution)/shard_map/pallas_call | solution.py:466
  73.6 1.4 %shard_map.94 = (bf16[128,4096]{1,0:T(8,128)(2,1)}, bf16[128,4096]{1,0:T(8,128)(2,1)}, f32[8,64]{1,0:T(8,128)}, f32[8,64]{1,0:T(8,128)}) custom-call(bf16[128,4096]{1,0:T(8,128)(2,1)S(1)} %get-tuple-element.12.refs_0_, bf16[128,4096]{1,0:T(8,128)(2,1)S(1)} %get-tuple-element.13.refs_1_, f32[8,64]{1,0:T(8,128)S(1)} %get-tuple-element.14.refs_2_, ...), custom_call_target="tpu_custom_call" | custom-call | tf_op jit(solution)/shard_map/pallas_call | solution.py:479
